TPU v7x, 32 devices: a whole 2x2x4 slice. The times are simulated.
32 devices in a mesh: batch: 8 (over z, x), blk: 4 (over y, core).
Axes of the slice: x: 2, y: 2, z: 4, core: 2. Of those that a mesh axis runs over, the one named last changes fastest.
Arguments:
- tokens: bfloat16 [8, 1024, 512], P('batch', 'blk'), may hold values from -6 to 6
- memory: bfloat16 [8, 1024, 512], P('batch', 'blk'), may hold values from -6 to 6
- lengths: int32 [8], P('batch'), may hold values from 769 to 1024, as said below
- targets: int32 [8, 1024], P('batch'), may hold values from 0 to 31999
- expert_ids: int32 [2, 8, 1024, 1], P(None, 'batch', 'blk'), may hold values from 0 to 3; in each aligned block of 256 rows (0 to 255, 256 to 511, ..., all dimensions but the last counted through in order) at most 96 rows name the same one
- gain_self: float32 [512], replicated, may hold values from 0.5 to 1.5
- gain_cross: float32 [512], replicated, may hold values from 0.5 to 1.5
- gain_ffn: float32 [512], replicated, may hold values from 0.5 to 1.5
- gain_out: float32 [512], replicated, may hold values from 0.5 to 1.5
- wq: bfloat16 [512, 512], replicated, may hold values from -0.25 to 0.25
- wk: bfloat16 [512, 512], replicated, may hold values from -0.25 to 0.25
- wv: bfloat16 [512, 512], replicated, may hold values from -0.25 to 0.25
- wo: bfloat16 [512, 512], replicated, may hold values from -0.75 to 0.75
- cq: bfloat16 [512, 512], replicated, may hold values from -0.25 to 0.25
- ck: bfloat16 [512, 512], replicated, may hold values from -0.25 to 0.25
- cv: bfloat16 [512, 512], replicated, may hold values from -0.25 to 0.25
- co: bfloat16 [512, 512], replicated, may hold values from -0.75 to 0.75
- w_in: bfloat16 [4, 512, 2048], P('blk'), may hold values from -0.25 to 0.25
- w_out: bfloat16 [4, 2048, 512], P('blk'), may hold values from -0.125 to 0.125
- embed: bfloat16 [32000, 512], P('blk'), may hold values from -0.5 to 0.5
Outputs:
- token_loss: float32 [8, 1024], P('batch', 'blk')
- grad_tokens: float32 [8, 1024, 512], P('batch', 'blk')
- grad_memory: float32 [8, 1024, 512], P('batch', 'blk')
- grad_gain_self: float32 [512], replicated
- grad_gain_cross: float32 [512], replicated
- grad_gain_ffn: float32 [512], replicated
- grad_gain_out: float32 [512], replicated
- grad_wq: float32 [512, 512], P('batch', 'blk')
- grad_wk: float32 [512, 512], P('batch', 'blk')
- grad_wv: float32 [512, 512], P('batch', 'blk')
- grad_wo: float32 [512, 512], P('batch', 'blk')
- grad_cq: float32 [512, 512], P('batch', 'blk')
- grad_ck: float32 [512, 512], P('batch', 'blk')
- grad_cv: float32 [512, 512], P('batch', 'blk')
- grad_co: float32 [512, 512], P('batch', 'blk')
- grad_w_in: float32 [4, 512, 2048], P('blk', 'batch')
- grad_w_out: float32 [4, 2048, 512], P('blk', 'batch')
- grad_embed: float32 [32000, 512], P('blk', 'batch')
Inputs may be any that keep to these rules, and one draw needn't show every extreme that they name: `lengths`: every sequence has live positions on the last device of its group (769 or more); some sequence is full. `expert_ids`: among the 256 tokens of one device in one pass, at most 96 name the same expert.
All inputs are finite; a program needn't handle non-finite values.
Results may differ from a plain program's by a relative error of at most 0.019.
Values may be sent and summed in bfloat16 or wider, within the bound.
No kernel may reach another device: no remote copies, remote signals or barrier semaphores. Data moves between devices by JAX's collectives and lax.ppermute only.
A program may use at most 384 MiB of HBM per device.

v0:
```python
import jax
import jax.numpy as jnp
from jax import lax
from jax.sharding import PartitionSpec as P

HEADS = 8
HD = 64


EPS_NORM = 1e-05
SMOOTH = 0.1


def combined_all(value, axis, join):
    pieces = jax.tree.map(lambda part: lax.all_gather(part, axis), value)
    head = jax.tree.map(lambda part: part[0], pieces)
    tail = jax.tree.map(lambda part: part[1:], pieces)
    total, _ = lax.scan(lambda total, slab: (join(total, slab), None), head, tail)
    return total


def norm_rows(values, gain):
    center = values - jnp.mean(values, axis=-1, keepdims=True)
    spread = jnp.mean(center * center, axis=-1, keepdims=True)
    return center * lax.rsqrt(spread + EPS_NORM) * gain


def norm_back(values, gain, upstream):
    _, pullback = jax.vjp(norm_rows, values, gain)
    return pullback(upstream)


def project(inputs, weight):
    return jnp.dot(inputs, weight, preferred_element_type=jnp.float32).astype(jnp.bfloat16)


def wide_product(form, left, right):
    return jnp.einsum(
        form, left.astype(jnp.float32), right.astype(jnp.float32), precision=lax.Precision.HIGHEST
    )


def split_heads(matrix):
    return matrix.reshape(matrix.shape[0], HEADS, HD).transpose(1, 0, 2)


def join_heads(stacked):
    return stacked.transpose(1, 0, 2).reshape(stacked.shape[1], HEADS * HD)


def head_scores(query_head, key_head, query_pos, causal):
    scores = jnp.einsum(
        "qd,kd->qk", query_head, key_head, preferred_element_type=jnp.float32
    ) * HD ** (-0.5)
    if causal:
        key_pos = jnp.arange(key_head.shape[0], dtype=jnp.int32)
        scores = jnp.where(key_pos[None, :] <= query_pos[:, None], scores, -1e30)
    return scores


def attend_heads(queries, keys, values, query_pos, causal):

    def one_head(operands):
        query_head, key_head, value_head = operands
        scores = head_scores(query_head, key_head, query_pos, causal)
        row_max = jnp.max(scores, axis=-1, keepdims=True)
        weights = jnp.exp(scores - row_max)
        row_total = jnp.sum(weights, axis=-1, keepdims=True)
        probs = (weights / row_total).astype(jnp.bfloat16)
        output = jnp.dot(probs, value_head, preferred_element_type=jnp.float32).astype(jnp.bfloat16)
        return (output, (row_max + jnp.log(row_total))[:, 0])

    outputs, log_totals = lax.map(
        one_head, (split_heads(queries), split_heads(keys), split_heads(values))
    )
    return (join_heads(outputs), log_totals)


def attend_back(queries, keys, values, log_totals, upstream, query_pos, causal):

    def one_head(operands):
        query_head, key_head, value_head, log_total, up_head = operands
        scores = head_scores(query_head, key_head, query_pos, causal)
        probs = jnp.exp(scores - log_total[:, None])
        grad_probs = jnp.einsum(
            "qd,kd->qk", up_head, value_head, preferred_element_type=jnp.float32
        )
        grad_value = jnp.einsum(
            "qk,qd->kd", probs.astype(jnp.bfloat16), up_head, preferred_element_type=jnp.float32
        )
        inner = jnp.sum(probs * grad_probs, axis=-1, keepdims=True)
        grad_scores = (probs * (grad_probs - inner)).astype(jnp.bfloat16)
        grad_query = jnp.dot(grad_scores, key_head, preferred_element_type=jnp.float32) * HD ** (
            -0.5
        )
        grad_key = jnp.einsum(
            "qk,qd->kd", grad_scores, query_head, preferred_element_type=jnp.float32
        ) * HD ** (-0.5)
        return (grad_query, grad_key, grad_value)

    operands = (
        split_heads(queries),
        split_heads(keys),
        split_heads(values),
        log_totals,
        split_heads(upstream),
    )
    grad_queries, grad_keys, grad_values = lax.map(one_head, operands)
    return (join_heads(grad_queries), join_heads(grad_keys), join_heads(grad_values))


def to_experts(grouped, experts_dev, group_size, count, model_width):
    return (
        grouped.reshape(2, group_size, experts_dev, count, model_width)
        .transpose(2, 0, 1, 3, 4)
        .reshape(experts_dev, 2 * group_size * count, model_width)
    )


def from_experts(stacked, experts_dev, group_size, count, model_width):
    return (
        stacked.reshape(experts_dev, 2, group_size, count, model_width)
        .transpose(1, 2, 0, 3, 4)
        .reshape(2, group_size * experts_dev, count, model_width)
    )


def per_device(
    tokens,
    memory,
    lengths,
    targets,
    expert_ids,
    gain_self,
    gain_cross,
    gain_ffn,
    gain_out,
    wq,
    wk,
    wv,
    wo,
    cq,
    ck,
    cv,
    co,
    w_in,
    w_out,
    embed,
):
    group_index = lax.axis_index("blk")
    group_size = lax.axis_size("blk")
    batch_size = lax.axis_size("batch")
    own_rows = tokens.shape[1]
    model_width = tokens.shape[2]
    own_states = tokens[0].astype(jnp.float32)
    own_memory = memory[0]
    query_pos = group_index * own_rows + jnp.arange(own_rows, dtype=jnp.int32)
    h_one = norm_rows(own_states, gain_self).astype(jnp.bfloat16)
    queries = project(h_one, wq)
    keys_own = project(h_one, wk)
    values_own = project(h_one, wv)
    memkey_own = project(own_memory, ck)
    memval_own = project(own_memory, cv)
    all_keys, all_values, mem_keys, mem_values = (
        lax.all_gather(keys_own, "blk", axis=0, tiled=True),
        lax.all_gather(values_own, "blk", axis=0, tiled=True),
        lax.all_gather(memkey_own, "blk", axis=0, tiled=True),
        lax.all_gather(memval_own, "blk", axis=0, tiled=True),
    )
    attn_out, self_lse = attend_heads(queries, all_keys, all_values, query_pos, True)
    middle = own_states + jnp.dot(attn_out, wo, preferred_element_type=jnp.float32)
    h_two = norm_rows(middle, gain_cross).astype(jnp.bfloat16)
    cross_q = project(h_two, cq)
    cross_out, cross_lse = attend_heads(cross_q, mem_keys, mem_values, query_pos, False)
    after_cross = middle + jnp.dot(cross_out, co, preferred_element_type=jnp.float32)
    h_three = norm_rows(after_cross, gain_ffn).astype(jnp.bfloat16)
    experts_dev = w_in.shape[0]
    experts_all = experts_dev * group_size
    capacity = 3 * own_rows // (2 * experts_all)
    picks = expert_ids[:, 0, :, 0]
    onehot = (picks[:, :, None] == jnp.arange(experts_all, dtype=jnp.int32)[None, None, :]).astype(
        jnp.int32
    )
    before = jnp.cumsum(onehot, axis=1) - onehot
    slot = jnp.sum(onehot * before, axis=-1)
    target_slot = picks * capacity + slot
    routing = (
        target_slot[:, None, :]
        == jnp.arange(experts_all * capacity, dtype=jnp.int32)[None, :, None]
    ).astype(jnp.bfloat16)
    send_rows = jnp.einsum(
        "psr,rd->psd", routing, h_three, preferred_element_type=jnp.float32
    ).astype(jnp.bfloat16)
    send_rows = send_rows.reshape(2, experts_all, capacity, model_width)
    arrived = lax.all_to_all(send_rows, "blk", split_axis=1, concat_axis=1, tiled=True)
    count = arrived.shape[2]
    grouped = to_experts(arrived, experts_dev, group_size, count, model_width)
    up_values = jnp.einsum("erd,edf->erf", grouped, w_in, preferred_element_type=jnp.float32)
    activity = jax.nn.gelu(up_values).astype(jnp.bfloat16)
    result = jnp.einsum("erf,efd->erd", activity, w_out, preferred_element_type=jnp.float32).astype(
        jnp.bfloat16
    )
    result = from_experts(result, experts_dev, group_size, count, model_width)
    returned = lax.all_to_all(result, "blk", split_axis=1, concat_axis=1, tiled=True)
    returned, arrived = (returned, arrived)
    expert_out = jnp.einsum(
        "psr,psd->prd",
        routing,
        returned.reshape(2, experts_all * capacity, model_width),
        preferred_element_type=jnp.float32,
    )
    outputs = after_cross[None] + expert_out
    z_pair = norm_rows(outputs, gain_out).astype(jnp.bfloat16)
    group_z = lax.all_gather(z_pair, "blk", axis=1, tiled=True)
    seq_len = group_z.shape[1]
    vocab_part = embed.shape[0]
    vocab_total = vocab_part * group_size
    vocab_ids = group_index * vocab_part + jnp.arange(vocab_part, dtype=jnp.int32)
    block = min(1024, seq_len)
    steps_count = seq_len // block
    z_blocks = group_z.reshape(2, steps_count, block, model_width).transpose(1, 0, 2, 3)
    labels = targets[0].reshape(steps_count, block)

    def partial_stats(operands):
        z_block, label_block = operands
        logit_pair = jnp.einsum("prd,vd->prv", z_block, embed, preferred_element_type=jnp.float32)
        difference = logit_pair[0] - logit_pair[1]
        row_max = jnp.max(logit_pair, axis=-1)
        weights = jnp.exp(logit_pair - row_max[..., None])
        row_total = jnp.sum(weights, axis=-1)
        weighted = jnp.sum(weights * difference[None], axis=-1)
        hits = (label_block[:, None] == vocab_ids[None, :]).astype(jnp.float32)
        picked = jnp.sum(logit_pair * hits[None], axis=-1)
        summed = jnp.sum(logit_pair, axis=-1)
        return (row_max, row_total, weighted, picked, summed)

    stats = lax.map(partial_stats, (z_blocks, labels))

    def join(first, second):
        max_one, total_one, weight_one, pick_one, sum_one = first
        max_two, total_two, weight_two, pick_two, sum_two = second
        joined_max = jnp.maximum(max_one, max_two)
        scale_one = jnp.exp(max_one - joined_max)
        scale_two = jnp.exp(max_two - joined_max)
        return (
            joined_max,
            total_one * scale_one + total_two * scale_two,
            weight_one * scale_one + weight_two * scale_two,
            pick_one + pick_two,
            sum_one + sum_two,
        )

    row_max, row_total, weighted, picked, summed = combined_all(stats, "blk", join)
    log_total = row_max + jnp.log(row_total)
    expect = weighted / row_total
    cross_entropy = log_total - (1.0 - SMOOTH) * picked - SMOOTH * summed / vocab_total
    live = (
        (jnp.arange(seq_len, dtype=jnp.int32) < lengths[0])
        .astype(jnp.float32)
        .reshape(steps_count, block)
    )
    losses = (
        live * (cross_entropy[:, 0] + cross_entropy[:, 1] + expect[:, 0] - expect[:, 1])
    ).reshape(seq_len)
    own_loss = lax.dynamic_slice_in_dim(losses, group_index * own_rows, own_rows)

    def grad_block(carry, operands):
        z_block, label_block, lse_block, expect_block, live_block = operands
        logit_pair = jnp.einsum("prd,vd->prv", z_block, embed, preferred_element_type=jnp.float32)
        probs = jnp.exp(logit_pair - lse_block[..., None])
        difference = logit_pair[0] - logit_pair[1]
        hits = (label_block[:, None] == vocab_ids[None, :]).astype(jnp.float32)
        smooth = (1.0 - SMOOTH) * hits + SMOOTH / vocab_total
        apart = probs[0] - probs[1]
        grad_zero = probs[0] - smooth + apart + probs[0] * (difference - expect_block[0][:, None])
        grad_one = probs[1] - smooth - apart - probs[1] * (difference - expect_block[1][:, None])
        grad_logits = (jnp.stack([grad_zero, grad_one]) * live_block[None, :, None]).astype(
            jnp.bfloat16
        )
        grad_z = jnp.einsum("prv,vd->prd", grad_logits, embed, preferred_element_type=jnp.float32)
        carry = carry + jnp.einsum(
            "prv,prd->vd", grad_logits, z_block, preferred_element_type=jnp.float32
        )
        return (carry, grad_z)

    embed_local, grad_z_blocks = lax.scan(
        grad_block,
        jnp.zeros((vocab_part, model_width), jnp.float32),
        (z_blocks, labels, log_total, expect, live),
    )
    grad_z_group = grad_z_blocks.transpose(1, 0, 2, 3).reshape(2, seq_len, model_width)
    grad_z_own = lax.psum_scatter(
        grad_z_group.astype(jnp.bfloat16), "blk", scatter_dimension=1, tiled=True
    ).astype(jnp.float32)
    grad_outputs, grad_gain_out = norm_back(outputs, gain_out, grad_z_own)
    send_grads = jnp.einsum(
        "psr,prd->psd",
        routing,
        grad_outputs.astype(jnp.bfloat16),
        preferred_element_type=jnp.float32,
    ).astype(jnp.bfloat16)
    send_grads = send_grads.reshape(2, experts_all, capacity, model_width)
    arrived_grads = lax.all_to_all(send_grads, "blk", split_axis=1, concat_axis=1, tiled=True)
    grouped = to_experts(arrived, experts_dev, group_size, capacity, model_width)
    grouped_grads = to_experts(arrived_grads, experts_dev, group_size, capacity, model_width)
    up_values = jnp.einsum("erd,edf->erf", grouped, w_in, preferred_element_type=jnp.float32)
    activity = jax.nn.gelu(up_values).astype(jnp.bfloat16)
    grad_activity = jnp.einsum(
        "erd,efd->erf", grouped_grads, w_out, preferred_element_type=jnp.float32
    )
    _, gelu_pull = jax.vjp(jax.nn.gelu, up_values)
    grad_up = gelu_pull(grad_activity)[0].astype(jnp.bfloat16)
    w_out_local = jnp.einsum(
        "erf,erd->efd", activity, grouped_grads, preferred_element_type=jnp.float32
    )
    w_in_local = jnp.einsum("erd,erf->edf", grouped, grad_up, preferred_element_type=jnp.float32)
    grad_rows = jnp.einsum("erf,edf->erd", grad_up, w_in, preferred_element_type=jnp.float32)
    grad_rows = from_experts(grad_rows, experts_dev, group_size, capacity, model_width)
    back_grads = lax.all_to_all(
        grad_rows.astype(jnp.bfloat16), "blk", split_axis=1, concat_axis=1, tiled=True
    ).astype(grad_rows.dtype)
    grad_h_three = jnp.einsum(
        "psr,psd->rd",
        routing.astype(jnp.float32),
        back_grads.reshape(2, experts_all * capacity, model_width),
    )
    norm_part, grad_gain_ffn = norm_back(after_cross, gain_ffn, grad_h_three)
    grad_after = grad_outputs[0] + grad_outputs[1] + norm_part
    branch_two = grad_after.astype(jnp.bfloat16)
    grad_co = jnp.einsum("rd,re->de", cross_out, branch_two, preferred_element_type=jnp.float32)
    grad_cross_out = jnp.einsum(
        "re,de->rd", branch_two, co, preferred_element_type=jnp.float32
    ).astype(jnp.bfloat16)
    grad_cross_q, memkey_part, memval_part = attend_back(
        cross_q, mem_keys, mem_values, cross_lse, grad_cross_out, query_pos, False
    )
    cross_q_low = grad_cross_q.astype(jnp.bfloat16)
    grad_cq = jnp.einsum("rd,re->de", h_two, cross_q_low, preferred_element_type=jnp.float32)
    grad_h_two = jnp.einsum("re,de->rd", cross_q_low, cq, preferred_element_type=jnp.float32)
    norm_part, grad_gain_cross = norm_back(middle, gain_cross, grad_h_two)
    grad_middle = grad_after + norm_part
    branch_one = grad_middle.astype(jnp.bfloat16)
    grad_wo = jnp.einsum("rd,re->de", attn_out, branch_one, preferred_element_type=jnp.float32)
    grad_attn_out = jnp.einsum(
        "re,de->rd", branch_one, wo, preferred_element_type=jnp.float32
    ).astype(jnp.bfloat16)
    grad_queries, key_part, value_part = attend_back(
        queries, all_keys, all_values, self_lse, grad_attn_out, query_pos, True
    )
    queries_low = grad_queries.astype(jnp.bfloat16)
    grad_wq = jnp.einsum("rd,re->de", h_one, queries_low, preferred_element_type=jnp.float32)
    grad_h_one = jnp.einsum("re,de->rd", queries_low, wq, preferred_element_type=jnp.float32)
    grad_keys, grad_values, grad_memkeys, grad_memvals = (
        lax.psum_scatter(
            key_part.astype(jnp.bfloat16), "blk", scatter_dimension=0, tiled=True
        ).astype(jnp.float32),
        lax.psum_scatter(
            value_part.astype(jnp.bfloat16), "blk", scatter_dimension=0, tiled=True
        ).astype(jnp.float32),
        lax.psum_scatter(
            memkey_part.astype(jnp.bfloat16), "blk", scatter_dimension=0, tiled=True
        ).astype(jnp.float32),
        lax.psum_scatter(
            memval_part.astype(jnp.bfloat16), "blk", scatter_dimension=0, tiled=True
        ).astype(jnp.float32),
    )
    own_key_term = wide_product("re,de->rd", grad_keys, wk) + wide_product(
        "re,de->rd", grad_values, wv
    )
    grad_wk = wide_product("rd,re->de", h_one, grad_keys)
    grad_wv = wide_product("rd,re->de", h_one, grad_values)
    grad_ck = wide_product("rd,re->de", own_memory, grad_memkeys)
    grad_cv = wide_product("rd,re->de", own_memory, grad_memvals)
    grad_memory = wide_product("re,de->rd", grad_memkeys, ck) + wide_product(
        "re,de->rd", grad_memvals, cv
    )
    grad_h_one = grad_h_one + own_key_term
    norm_part, grad_gain_self = norm_back(own_states, gain_self, grad_h_one)
    grad_tokens = grad_middle + norm_part
    stacked_weights = jnp.stack(
        [grad_wq, grad_wk, grad_wv, grad_wo, grad_cq, grad_ck, grad_cv, grad_co]
    )
    row_part = model_width // batch_size
    col_part = model_width // group_size
    tiled = (
        stacked_weights.reshape(8, batch_size, row_part, group_size, col_part)
        .transpose(0, 1, 3, 2, 4)
        .reshape(8, model_width * model_width)
    )
    summed_flat = lax.psum_scatter(tiled, ("batch", "blk"), scatter_dimension=1, tiled=True)
    summed_weights = summed_flat.reshape(8, row_part, col_part)
    stacked_gains = jnp.stack([grad_gain_self, grad_gain_cross, grad_gain_ffn, grad_gain_out])
    summed_gains = lax.psum(stacked_gains, ("batch", "blk"))
    w_in_sum, w_out_sum, embed_sum = (
        lax.psum_scatter(
            w_in_local.astype(jnp.bfloat16), "batch", scatter_dimension=1, tiled=True
        ).astype(jnp.float32),
        lax.psum_scatter(
            w_out_local.astype(jnp.bfloat16), "batch", scatter_dimension=1, tiled=True
        ).astype(jnp.float32),
        lax.psum_scatter(
            embed_local.astype(jnp.bfloat16), "batch", scatter_dimension=1, tiled=True
        ).astype(jnp.float32),
    )
    return (
        own_loss[None],
        grad_tokens[None],
        grad_memory[None],
        summed_gains[0],
        summed_gains[1],
        summed_gains[2],
        summed_gains[3],
        summed_weights[0],
        summed_weights[1],
        summed_weights[2],
        summed_weights[3],
        summed_weights[4],
        summed_weights[5],
        summed_weights[6],
        summed_weights[7],
        w_in_sum,
        w_out_sum,
        embed_sum,
    )


def solution(mesh):
    return jax.shard_map(
        per_device,
        mesh=mesh,
        in_specs=(
            P("batch", "blk", None),
            P("batch", "blk", None),
            P("batch"),
            P("batch", None),
            P(None, "batch", "blk", None),
            P(),
            P(),
            P(),
            P(),
            P(),
            P(),
            P(),
            P(),
            P(),
            P(),
            P(),
            P(),
            P("blk", None, None),
            P("blk", None, None),
            P("blk", None),
        ),
        out_specs=(
            P("batch", "blk"),
            P("batch", "blk", None),
            P("batch", "blk", None),
            P(),
            P(),
            P(),
            P(),
            P("batch", "blk"),
            P("batch", "blk"),
            P("batch", "blk"),
            P("batch", "blk"),
            P("batch", "blk"),
            P("batch", "blk"),
            P("batch", "blk"),
            P("batch", "blk"),
            P("blk", "batch", None),
            P("blk", "batch", None),
            P("blk", "batch"),
        ),
        check_vma=False,
    )
```

profile of v0, /device:TPU:0, one launch (start us, length us, event | category | flops | bytes accessed | tf_op | source)
XLA Modules:
  0.0 1242.6 jit_solution(5317219785034045139)
XLA Ops:
  20.1 2.4 reduce-window.6
  23.8 7.7 all-gather.16.cloned.1.call-done
  33.8 2.8 copy.144
  36.6 13.9 %all-gather.18.cloned.1.call-done = bf16[1024,512]{1,0:T(8,128)(2,1)} async-done(((bf16[256,512]{1,0:T(8,128)(2,1)}), bf16[1024,512]{1,0:T(8,128)(2,1)}) %all-gather.18.cloned.1.call-update) | async-done | bytes 1048592 | tf_op jit(solution)/shard_map/all_gather | solution.py:166
  52.7 2.7 copy.145
  55.4 24.9 %while.88 = (s32[]{:T(128)}, bf16[8,256,64]{1,2,0:T(8,128)(2,1)S(1)}, f32[8,256]{1,0:T(8,128)S(1)}, bf16[8,256,64]{2,1,0:T(8,128)(2,1)S(1)}, bf16[8,1024,64]{2,1...) while((s32[]{:T(128)}, ...), condition=%wide.region_5.6_spmd.clone, body=%wide.region_2.5_spmd.clone.sunk | while | flops 69484544 | bytes 3782765 | solution.py:73
  88.1 2.7 copy.150
  93.2 2.8 copy.151
  96.0 24.6 %while.29 = (s32[]{:T(128)}, bf16[8,256,64]{1,2,0:T(8,128)(2,1)S(1)}, f32[8,256]{1,0:T(8,128)S(1)}, bf16[8,256,64]{2,1,0:T(8,128)(2,1)S(1)}, bf16[8,1024,64]{2,1...) while((s32[]{:T(128)}, bf16[8,256,64]{1,2,0:T(8,128)(2,1)S(1)}, ...), condition=%wide.region_11.12_spmd, body=%wide.region_8.11_spmd.sunk | while | flops 68960000 | bytes 3780705 | solution.py:73
  123.3 14.1 %all_to_all.20 = bf16[2,4,96,512]{3,2,0,1:T(8,128)(2,1)S(1)} all-to-all(bf16[2,4,96,512]{3,2,0,1:T(8,128)(2,1)S(1)} %copy.155), channel_id=1, replica_groups=mesh['batch'=8,'blk'=4] {'blk'}, dimensions={1} | all-to-all | bytes 1572864 | tf_op jit(solution)/shard_map/all_to_all | solution.py:195
  140.2 2.4 fusion.112
  142.9 14.3 %all_to_all.21 = bf16[2,4,96,512]{3,2,0,1:T(8,128)(2,1)S(1)} all-to-all(bf16[2,4,96,512]{3,2,0,1:T(8,128)(2,1)S(1)} %copy.157), channel_id=1, replica_groups=mesh['batch'=8,'blk'=4] {'blk'}, dimensions={1} | all-to-all | bytes 1572864 | tf_op jit(solution)/shard_map/all_to_all | solution.py:204
  161.8 11.4 compare_convert_fusion
  173.1 10.0 all-gather.24.cloned.1.call-done
  183.2 30.3 %fusion.200 = (f32[2,1024]{1,0:T(2,128)S(1)}, f32[2,1024,8000]{1,2,0:T(8,128)}) fusion(bf16[2,1024,512]{2,1,0:T(8,128)(2,1)} %all-gather.24.cloned.1.call-done, bf16[8000,512]{1,0:T(8,128)(2,1)} %param.49), kind=kOutput, calls=%fused_computation.324 | convolution fusion | flops 16793597952 | bytes 75833344 | tf_op jit(solution)/shard_map/while/body/eval_jaxpr/prd,vd->prv/dot_general | solution.py:226
  213.5 5.2 all-gather.5
  218.6 32.4 %fusion.187 = f32[1024,8000]{0,1:T(8,128)} fusion(f32[2,1024,8000]{1,2,0:T(8,128)} %get-tuple-element.636), kind=kLoop, calls=%fused_computation.312 | loop fusion | flops 8192000 | bytes 98304000 | tf_op jit(solution)/shard_map/while/body/eval_jaxpr/mul | solution.py:231
  251.0 40.6 %fusion.188 = (f32[2,1024]{1,0:T(2,128)S(1)}, f32[2,1024]{1,0:T(2,128)S(1)}, f32[2,1024]{1,0:T(2,128)S(1)}, f32[2,1024]{1,0:T(2,128)S(1)}) fusion(f32[2,1024,8000]{1,2,0:T(8,128)} %get-tuple-element.636, f32[1024,8000]{0,1:T(8,128)} %compare_convert_fusion, f32[2,1024]{1,0:T(2,128)S(1)} %get-tuple-element.635, f32[1024,8000]{0,1:T(8,128)} %fusion.187), kind=kLoop, calls=%fused_computation.313 | loop fusion | flops 114679808 | bytes 131112960 | tf_op jit(solution)/shard_map/while/body/eval_jaxpr/reduce_sum | solution.py:234
  291.7 5.2 all-gather.6
  296.9 5.2 all-gather.7
  302.0 5.2 all-gather.8
  307.2 5.6 all-gather.9
  313.2 43.4 %subtract_exponential_fusion.3 = f32[2,1024,8000]{1,2,0:T(8,128)} fusion(f32[2,1024,8000]{1,2,0:T(8,128)} %get-tuple-element.636, f32[2,1024]{1,0:T(2,128)S(1)} %get-tuple-element.619), kind=kLoop, calls=%fused_computation.122 | loop fusion | flops 16384000 | bytes 131080192 | tf_op jit(solution)/shard_map/while/body/eval_jaxpr/exp | solution.py:270
  357.2 62.8 %multiply_add_fusion = (f32[1,1024,8000]{1,2,0:T(8,128)}, f32[1,1024,8000]{1,2,0:T(8,128)}) fusion(f32[2,1024,8000]{1,2,0:T(8,128)} %subtract_exponential_fusion.3, f32[1024]{0:T(1024)S(1)} %bitcast.648, s32[1024]{0:T(1024)S(1)} %bitcast.647, s32[8000]{0:T(1024)S(1)} %iota_add_fusion.2, f32[2,1024,8000]{1,2,0:T(8,128)} %get-tuple-element.636, ...), kind=kLoop, calls=%fused_computation.129 | loop fusion | flops 122880000 | bytes 196652288 | tf_op jit(solution)/shard_map/while/body/eval_jaxpr/add | solution.py:275
  420.1 29.0 %fusion.109 = bf16[2,1024,512]{2,1,0:T(8,128)(2,1)} fusion(bf16[8000,512]{1,0:T(8,128)(2,1)} %param.49, f32[1,1024,8000]{1,2,0:T(8,128)} %get-tuple-element.607, f32[1,1024,8000]{1,2,0:T(8,128)} %get-tuple-element.606, f32[1024]{0:T(1024)S(1)} %copy-done.72), kind=kOutput, calls=%fused_computation.160 | convolution fusion | flops 16827416576 | bytes 75829248 | tf_op jit(solution)/shard_map/while/body/eval_jaxpr/prv,vd->prd/dot_general | solution.py:280
  449.1 31.6 %reduce-scatter.10.cloned.1.call-done = bf16[2,256,512]{2,1,0:T(8,128)(2,1)} async-done(((bf16[2,1024,512]{2,1,0:T(8,128)(2,1)}), bf16[2,256,512]{2,1,0:T(8,128)(2,1)}) %reduce-scatter.10.cloned.1.call-update) | async-done | bytes 524304 | tf_op jit(solution)/shard_map/reduce_scatter | solution.py:292
  486.6 14.2 %all_to_all.22 = bf16[2,4,96,512]{3,2,0,1:T(8,128)(2,1)S(1)} all-to-all(bf16[2,4,96,512]{3,2,0,1:T(8,128)(2,1)S(1)} %copy.165), channel_id=1, replica_groups=mesh['batch'=8,'blk'=4] {'blk'}, dimensions={1} | all-to-all | bytes 1572864 | tf_op jit(solution)/shard_map/all_to_all | solution.py:303
  500.9 7.3 fusion.99
  512.8 3.5 all-to-all-start.3
  516.4 11.6 all-to-all-done.3
  535.2 66.2 %while.87 = (s32[]{:T(128)}, bf16[8,256,64]{1,2,0:T(8,128)(2,1)S(1)}, bf16[8,1024,64]{1,2,0:T(8,128)(2,1)}, bf16[8,1024,64]{1,2,0:T(8,128)(2,1)}, bf16[8,256,64]...) while((s32[]{:T(128)}, ...), condition=%wide.region_33.34_spmd, body=%wide.region_31.33_spmd.sunk | while | flops 169950976 | bytes 9447537 | solution.py:108
  610.0 71.9 %while.89 = (s32[]{:T(128)}, bf16[8,256,64]{1,2,0:T(8,128)(2,1)}, bf16[8,1024,64]{1,2,0:T(8,128)(2,1)}, bf16[8,1024,64]{1,2,0:T(8,128)(2,1)}, bf16[8,256,64]{2,1...) while((s32[]{:T(128)}, bf16[8,256,64]{1,2,0:T(8,128)(2,1)}, ...), condition=%wide.region_38.39_spmd.clone, body=%wide.region_36.38_spmd.clone.sunk | while | flops 170475520 | bytes 9449597 | solution.py:108
  684.1 5.1 fusion.100
  689.4 7.1 fusion.101
  696.6 30.1 %bitcast_convert_fusion = bf16[8000,512]{0,1:T(8,128)(2,1)} fusion(bf16[2,1024,512]{2,1,0:T(8,128)(2,1)} %all-gather.24.cloned.1.call-done, f32[1,1024,8000]{1,2,0:T(8,128)} %get-tuple-element.607, f32[1,1024,8000]{1,2,0:T(8,128)} %get-tuple-element.606, f32[1024]{0:T(1024)S(1)} %copy-done.72), kind=kOutput, calls=%fused_computation.133 | convolution fusion | flops 16830464000 | bytes 75829248 | tf_op jit(solution)/shard_map/while/body/eval_jaxpr/prv,prd->vd/dot_general | solution.py:281
  746.8 15.7 %reduce-scatter.16.cloned.1.call-done = bf16[256,512]{0,1:T(8,128)(2,1)} async-done(((bf16[1024,512]{0,1:T(8,128)(2,1)}), bf16[256,512]{0,1:T(8,128)(2,1)}) %reduce-scatter.16.cloned.1.call-update) | async-done | bytes 262160 | tf_op jit(solution)/shard_map/reduce_scatter | solution.py:360
  767.8 22.0 %reduce-scatter.18.cloned.1.call-done = bf16[256,512]{0,1:T(8,128)(2,1)} async-done(((bf16[1024,512]{0,1:T(8,128)(2,1)}), bf16[256,512]{0,1:T(8,128)(2,1)}) %reduce-scatter.18.cloned.1.call-update) | async-done | bytes 262160 | tf_op jit(solution)/shard_map/reduce_scatter | solution.py:363
  792.2 2.7 reshape.745
  794.9 3.2 copy.187
  798.1 2.4 fusion.122
  805.2 2.4 fusion.119
  811.1 10.7 copy.212
  823.2 39.9 %psum.7 = f32[4,512]{1,0:T(4,128)S(1)} all-reduce(f32[4,512]{1,0:T(4,128)S(1)} %pad_maximum_fusion), channel_id=1, replica_groups=mesh['batch'=8,'blk'=4] {'batch','blk'}, use_global_device_ids=true, to_apply=%region_49.50 | all-reduce | flops 2048 | bytes 16384 | tf_op jit(solution)/shard_map/psum | solution.py:393
  867.9 64.5 %reduce-scatter.24.cloned.1.call-done = bf16[1,256,512]{2,1,0:T(8,128)(2,1)} async-done(((bf16[1,2048,512]{2,1,0:T(8,128)(2,1)}), bf16[1,256,512]{2,1,0:T(8,128)(2,1)}) %reduce-scatter.24.cloned.1.call-update) | async-done | bytes 262160 | tf_op jit(solution)/shard_map/reduce_scatter | solution.py:398
  934.2 148.1 %reduce-scatter.26.cloned.1.call-done = bf16[8000,64]{0,1:T(8,128)(2,1)} async-done(((bf16[8000,512]{0,1:T(8,128)(2,1)}), bf16[8000,64]{0,1:T(8,128)(2,1)}) %reduce-scatter.26.cloned.1.call-update) | async-done | bytes 1024016 | tf_op jit(solution)/shard_map/reduce_scatter | solution.py:401
  1082.4 2.7 convert_element_type.286
  1085.0 147.6 %reduce-scatter.20.cloned.1.call-done = f32[8,8192]{1,0:T(8,128)} async-done(((f32[8,262144]{1,0:T(8,128)}), f32[8,8192]{1,0:T(8,128)}) %reduce-scatter.20.cloned.1.call-update) | async-done | bytes 262160 | tf_op jit(solution)/shard_map/reduce_scatter | solution.py:390
  1232.7 2.9 fusion.194
  (527 shorter events, 298.4 us)
Async XLA Ops:
  7.2 133.0 %copy-start = (bf16[1,2048,512]{2,1,0:T(8,128)(2,1)S(1)}, bf16[1,2048,512]{2,1,0:T(8,128)(2,1)}, u32[]{:S(2)}) copy-start(bf16[1,2048,512]{2,1,0:T(8,128)(2,1)} %param.48) | copy-start | bytes 6291460
  7.3 24.3 %all-gather.16.cloned.1.call-start = ((), (), s32[]{:S(2)}) async-start(), calls=%async_computation.13 | async-start | bytes 1310720 | tf_op jit(solution)/shard_map/all_gather | solution.py:165
  9.7 26.8 %copy-start.56 = (f32[256]{0:T(256)}, f32[256]{0:T(256)S(1)}, u32[]{:S(2)}) copy-start(f32[256]{0:T(256)S(1)} %fusion.175) | copy-start | bytes 3076
  12.0 38.5 %all-gather.18.cloned.1.call-start = ((), (), s32[]{:S(2)}) async-start(), calls=%async_computation.14 | async-start | bytes 1310720 | tf_op jit(solution)/shard_map/all_gather | solution.py:166
  14.2 71.6 %all-gather.20.cloned.1.call-start = ((), (), s32[]{:S(2)}) async-start(), calls=%async_computation.15 | async-start | bytes 1310720 | tf_op jit(solution)/shard_map/all_gather | solution.py:167
  16.4 74.5 %all-gather.22.cloned.1.call-start = ((), (), s32[]{:S(2)}) async-start(), calls=%async_computation.16 | async-start | bytes 1310720 | tf_op jit(solution)/shard_map/all_gather | solution.py:168
  18.6 164.5 %all-gather.24.cloned.1.call-start = ((), (), s32[]{:S(2)}) async-start(), calls=%async_computation.17 | async-start | bytes 2621440 | tf_op jit(solution)/shard_map/all_gather | solution.py:214
  23.0 134.3 %copy-start.42 = (s32[2,256]{1,0:T(2,128)}, s32[2,256]{1,0:T(2,128)S(1)}, u32[]{:S(2)}) copy-start(s32[2,256]{1,0:T(2,128)S(1)} %multiply_add_fusion.2) | copy-start | bytes 6148
  55.4 28.6 %copy-start.53 = (f32[512]{0:T(512)S(1)}, f32[512]{0:T(512)}, u32[]{:S(2)}) copy-start(f32[512]{0:T(512)} %param.36) | copy-start | bytes 6148
  82.7 37.9 %copy-start.3 = (f32[256,512]{1,0:T(8,128)}, f32[256,512]{1,0:T(8,128)S(1)}, u32[]{:S(2)}) copy-start(f32[256,512]{1,0:T(8,128)S(1)} %get-tuple-element.630) | copy-start | bytes 1572868
  96.0 26.6 %copy-start.70 = (f32[512]{0:T(512)S(1)}, f32[512]{0:T(512)}, u32[]{:S(2)}) copy-start(f32[512]{0:T(512)} %param.37) | copy-start | bytes 6148
  120.5 19.6 %copy-start.14 = (bf16[8,256,64]{2,1,0:T(8,128)(2,1)}, bf16[8,256,64]{2,1,0:T(8,128)(2,1)S(1)}, u32[]{:S(2)}) copy-start(bf16[8,256,64]{2,1,0:T(8,128)(2,1)S(1)} %get-tuple-element.1103) | copy-start | bytes 786436
  120.6 19.6 %copy-start.19 = (bf16[8,256,64]{1,2,0:T(8,128)(2,1)}, bf16[8,256,64]{1,2,0:T(8,128)(2,1)S(1)}, u32[]{:S(2)}) copy-start(bf16[8,256,64]{1,2,0:T(8,128)(2,1)S(1)} %get-tuple-element.314) | copy-start | bytes 786436
  120.6 19.6 %copy-start.49 = (f32[8,256]{1,0:T(8,128)}, f32[8,256]{1,0:T(8,128)S(1)}, u32[]{:S(2)}) copy-start(f32[8,256]{1,0:T(8,128)S(1)} %get-tuple-element.1021) | copy-start | bytes 24580
  122.3 34.9 %copy-start.5 = (f32[256,512]{1,0:T(8,128)}, f32[256,512]{1,0:T(8,128)S(1)}, u32[]{:S(2)}) copy-start(f32[256,512]{1,0:T(8,128)S(1)} %get-tuple-element.632) | copy-start | bytes 1572868
  142.9 18.9 %copy-start.55 = (s32[1,1024]{1,0:T(1,128)S(1)}, s32[1,1024]{1,0:T(1,128)}, u32[]{:S(2)}) copy-start(s32[1,1024]{1,0:T(1,128)} %param.33) | copy-start | bytes 12292
  160.4 320.2 %reduce-scatter.10.cloned.1.call-start = ((), (), s32[]{:S(2)}) async-start(), calls=%async_computation.18 | async-start | bytes 2621440 | tf_op jit(solution)/shard_map/reduce_scatter | solution.py:292
  357.2 62.8 %copy-start.72 = (f32[1024]{0:T(1024)S(1)}, f32[1024]{0:T(1024)}, u32[]{:S(2)}) copy-start(f32[1024]{0:T(1024)} %fusion.172) | copy-start | bytes 12292
  420.0 60.6 %copy-start.2 = (f32[2,256,512]{2,1,0:T(8,128)S(1)}, f32[2,256,512]{2,1,0:T(8,128)}, u32[]{:S(2)}) copy-start(f32[2,256,512]{2,1,0:T(8,128)} %copy-done.1) | copy-start | bytes 3145732
  420.0 60.6 %copy-start.35 = (f32[2,256]{1,0:T(2,128)S(1)}, f32[2,256]{1,0:T(2,128)}, u32[]{:S(2)}) copy-start(f32[2,256]{1,0:T(2,128)} %copy-done.34) | copy-start | bytes 6148
  420.1 60.6 %copy-start.41 = (f32[512]{0:T(512)S(1)}, f32[512]{0:T(512)}, u32[]{:S(2)}) copy-start(f32[512]{0:T(512)} %param.38) | copy-start | bytes 6148
  420.1 61.9 %copy-start.51 = (f32[2,256]{1,0:T(2,128)S(1)}, f32[2,256]{1,0:T(2,128)}, u32[]{:S(2)}) copy-start(f32[2,256]{1,0:T(2,128)} %copy-done.50) | copy-start | bytes 6148
  420.1 61.9 %copy-start.45 = (f32[2,256]{1,0:T(2,128)S(1)}, f32[2,256]{1,0:T(2,128)}, u32[]{:S(2)}) copy-start(f32[2,256]{1,0:T(2,128)} %copy-done.44) | copy-start | bytes 6148
  449.1 37.0 %copy-start.43 = (s32[2,256]{1,0:T(2,128)S(1)}, s32[2,256]{1,0:T(2,128)}, u32[]{:S(2)}) copy-start(s32[2,256]{1,0:T(2,128)} %copy-done.42) | copy-start | bytes 6148
  510.0 18.1 %copy-start.6 = (f32[256,512]{1,0:T(8,128)S(1)}, f32[256,512]{1,0:T(8,128)}, u32[]{:S(2)}) copy-start(f32[256,512]{1,0:T(8,128)} %copy-done.5) | copy-start | bytes 1572868
  510.0 18.1 %copy-start.61 = (f32[256]{0:T(256)S(1)}, f32[256]{0:T(256)}, u32[]{:S(2)}) copy-start(f32[256]{0:T(256)} %copy-done.60) | copy-start | bytes 3076
  510.0 18.1 %copy-start.63 = (f32[256]{0:T(256)S(1)}, f32[256]{0:T(256)}, u32[]{:S(2)}) copy-start(f32[256]{0:T(256)} %copy-done.62) | copy-start | bytes 3076
  510.0 18.1 %copy-start.71 = (f32[512]{0:T(512)S(1)}, f32[512]{0:T(512)}, u32[]{:S(2)}) copy-start(f32[512]{0:T(512)} %param.37) | copy-start | bytes 6148
  510.0 18.6 %copy-start.69 = (f32[256]{0:T(256)S(1)}, f32[256]{0:T(256)}, u32[]{:S(2)}) copy-start(f32[256]{0:T(256)} %copy-done.68) | copy-start | bytes 3076
  512.8 15.1 %all-to-all-start.3 = ((bf16[2,4,96,512]{3,2,0,1:T(8,128)(2,1)}), bf16[2,4,96,512]{3,2,0,1:T(8,128)(2,1)S(1)}, u32[]{:S(2)}, u32[]{:S(2)}) async-start(bf16[2,4,96,512]{3,2,0,1:T(8,128)(2,1)} %copy.167), calls=%async_computation.4 | async-start | bytes 1572864 | tf_op jit(solution)/shard_map/all_to_all | solution.py:319
  516.3 223.0 %reduce-scatter.12.cloned.1.call-start = ((), (), s32[]{:S(2)}) async-start(), calls=%async_computation.19 | async-start | bytes 1310720 | tf_op jit(solution)/shard_map/reduce_scatter | solution.py:354
  535.2 66.3 %copy-start.4 = (f32[256,512]{1,0:T(8,128)S(1)}, f32[256,512]{1,0:T(8,128)}, u32[]{:S(2)}) copy-start(f32[256,512]{1,0:T(8,128)} %copy-done.3) | copy-start | bytes 1572868
  535.2 66.3 %copy-start.26 = (bf16[512,512]{1,0:T(8,128)(2,1)S(1)}, bf16[512,512]{1,0:T(8,128)(2,1)}, u32[]{:S(2)}) copy-start(bf16[512,512]{1,0:T(8,128)(2,1)} %param.43) | copy-start | bytes 1572868
  535.2 66.3 %copy-start.47 = (f32[256]{0:T(256)S(1)}, f32[256]{0:T(256)}, u32[]{:S(2)}) copy-start(f32[256]{0:T(256)} %copy-done.46) | copy-start | bytes 3076
  535.2 66.3 %copy-start.54 = (f32[512]{0:T(512)S(1)}, f32[512]{0:T(512)}, u32[]{:S(2)}) copy-start(f32[512]{0:T(512)} %param.36) | copy-start | bytes 6148
  535.2 66.3 %copy-start.59 = (f32[256]{0:T(256)S(1)}, f32[256]{0:T(256)}, u32[]{:S(2)}) copy-start(f32[256]{0:T(256)} %copy-done.58) | copy-start | bytes 3076
  535.2 66.8 %copy-start.67 = (f32[256]{0:T(256)S(1)}, f32[256]{0:T(256)}, u32[]{:S(2)}) copy-start(f32[256]{0:T(256)} %copy-done.66) | copy-start | bytes 3076
  610.0 74.1 %copy-start.11 = (bf16[2,4,96,512]{3,2,1,0:T(8,128)(2,1)S(1)}, bf16[2,4,96,512]{3,2,1,0:T(8,128)(2,1)}, u32[]{:S(2)}) copy-start(bf16[2,4,96,512]{3,2,1,0:T(8,128)(2,1)} %copy-done.10) | copy-start | bytes 2359300
  681.9 59.7 %reduce-scatter.14.cloned.1.call-start = ((), (), s32[]{:S(2)}) async-start(), calls=%async_computation.20 | async-start | bytes 1310720 | tf_op jit(solution)/shard_map/reduce_scatter | solution.py:357
  682.7 79.9 %reduce-scatter.16.cloned.1.call-start = ((), (), s32[]{:S(2)}) async-start(), calls=%async_computation.21 | async-start | bytes 1310720 | tf_op jit(solution)/shard_map/reduce_scatter | solution.py:360
  683.4 106.4 %reduce-scatter.18.cloned.1.call-start = ((), (), s32[]{:S(2)}) async-start(), calls=%async_computation.22 | async-start | bytes 1310720 | tf_op jit(solution)/shard_map/reduce_scatter | solution.py:363
  684.0 182.1 %reduce-scatter.22.cloned.1.call-start = ((), (), s32[]{:S(2)}) async-start(), calls=%async_computation.24 | async-start | bytes 2359296 | tf_op jit(solution)/shard_map/reduce_scatter | solution.py:395
  689.2 243.2 %reduce-scatter.24.cloned.1.call-start = ((), (), s32[]{:S(2)}) async-start(), calls=%async_computation.25 | async-start | bytes 2359296 | tf_op jit(solution)/shard_map/reduce_scatter | solution.py:398
  696.6 385.8 %reduce-scatter.26.cloned.1.call-start = ((), (), s32[]{:S(2)}) async-start(), calls=%async_computation.26 | async-start | bytes 9289728 | tf_op jit(solution)/shard_map/reduce_scatter | solution.py:401
  726.8 505.9 %reduce-scatter.20.cloned.1.call-start = ((), (), s32[]{:S(2)}) async-start(), calls=%async_computation.23 | async-start | bytes 8650752 | tf_op jit(solution)/shard_map/reduce_scatter | solution.py:390
  821.8 41.3 %copy-start.25 = (bf16[512,512]{1,0:T(8,128)(2,1)S(1)}, bf16[512,512]{1,0:T(8,128)(2,1)}, u32[]{:S(2)}) copy-start(bf16[512,512]{1,0:T(8,128)(2,1)} %param.44) | copy-start | bytes 1572868
  821.8 41.3 %copy-start.30 = (bf16[256,512]{0,1:T(8,128)(2,1)S(1)}, bf16[256,512]{0,1:T(8,128)(2,1)}, u32[]{:S(2)}) copy-start(bf16[256,512]{0,1:T(8,128)(2,1)} %reduce-scatter.16.cloned.1.call-done) | copy-start | bytes 786436
  821.8 41.6 %copy-start.24 = (bf16[512,512]{1,0:T(8,128)(2,1)S(1)}, bf16[512,512]{1,0:T(8,128)(2,1)}, u32[]{:S(2)}) copy-start(bf16[512,512]{1,0:T(8,128)(2,1)} %param.45) | copy-start | bytes 1572868
  (40 other events, 277.1 us)
Sparse Core Ops, SparseCore 0:
  12.1 19.4 all-gather.15
  33.7 16.7 all-gather.17
  52.6 16.7 all-gather.19
  70.7 16.8 all-gather.21
  160.6 22.5 all-gather.23
  449.2 31.4 reduce-scatter.9
  682.1 24.8 reduce-scatter.11
  709.5 24.8 reduce-scatter.13
  737.7 24.8 reduce-scatter.15
  764.9 24.8 reduce-scatter.17
  793.8 67.8 reduce-scatter.21
  865.6 66.8 reduce-scatter.23
  936.6 145.7 reduce-scatter.25
  1084.6 148.0 reduce-scatter.19
where the time goes:
time: 1260 us; the launch traced here: 1240 us
  waiting for transfers between devices  475 us (38%)
  matrix products  326 us (26%)
  other arithmetic  227 us (18%)
  blocking collectives  109 us (9%)
  local copies, waits for them, and re-layouts  85 us (7%)
  between operations  16.1 us (1%)
    reduce_scatter x1, waiting for transfers between devices, per_device(): lax.psum_scatter(embed_local.astype(jnp.bfloat16), 'batch', scatter_dimen...  148 us
    reduce_scatter x1, waiting for transfers between devices, per_device(): lax.psum_scatter(tiled, ('batch', 'blk'), scatter_dimension=1, tiled=True)  148 us
    reduce_scatter x1, waiting for transfers between devices, per_device(): lax.psum_scatter(w_out_local.astype(jnp.bfloat16), 'batch', scatter_dimen...  64.5 us
    add x1, other arithmetic, grad_block(): probs[0] - smooth + apart  62.8 us
    dot_general x32, matrix products, head_scores(): jnp.einsum('qd,kd->qk', query_head, key_head, preferred_element_type=jnp....  45.8 us
    exp x1, other arithmetic, grad_block(): probs = jnp.exp(logit_pair - lse_block[..., None])  43.4 us
    reduce_sum x1, other arithmetic, partial_stats(): summed = jnp.sum(logit_pair, axis=-1)  40.6 us
    psum x1, blocking collectives, per_device(): summed_gains = lax.psum(stacked_gains, ('batch', 'blk'))  39.9 us
  transfers between devices with their start and end apart: 15, of which 10 were waited for; matrix products, arithmetic and copies ran while one was open for 14% of the time, Pallas kernels for 0%

commit v1 on v0

--- a/solution.py
+++ b/solution.py
@@ -1,6 +1,10 @@
+import functools
+
 import jax
 import jax.numpy as jnp
 from jax import lax
+from jax.experimental import pallas as pl
+from jax.experimental.pallas import tpu as pltpu
 from jax.sharding import PartitionSpec as P
 
 HEADS = 8
@@ -9,14 +13,272 @@
 
 EPS_NORM = 1e-05
 SMOOTH = 0.1
-
-
-def combined_all(value, axis, join):
-    pieces = jax.tree.map(lambda part: lax.all_gather(part, axis), value)
-    head = jax.tree.map(lambda part: part[0], pieces)
-    tail = jax.tree.map(lambda part: part[1:], pieces)
-    total, _ = lax.scan(lambda total, slab: (join(total, slab), None), head, tail)
-    return total
+LOG2E = 1.4426950408889634
+NN = (((1,), (0,)), ((), ()))
+NT = (((1,), (1,)), ((), ()))
+
+
+def dot(left, right, dims):
+    return lax.dot_general(left, right, dims, preferred_element_type=jnp.float32)
+
+
+def swap(value, axis, mask):
+    size = lax.axis_size(axis)
+    return lax.ppermute(value, axis, [(i, i ^ mask) for i in range(size)])
+
+
+def gather_blocks(own, axis):
+    size = lax.axis_size(axis)
+    blocks = {0: own}
+    bit = 2
+    while bit < size:
+        for k in range(0, bit, 2):
+            blocks[bit | k] = swap(blocks[k], axis, bit)
+        bit *= 2
+    for k in range(0, size, 2):
+        blocks[k | 1] = swap(blocks[k], axis, 1)
+    return [blocks[j] for j in range(size)]
+
+
+def scatter_blocks(parts, axis):
+    parts = list(parts)
+    size = len(parts)
+    bit = 1
+    while bit < size:
+        odd = [j for j in range(0, size, bit) if j & bit]
+        even = [j ^ bit for j in odd]
+        moved = swap(jnp.stack([parts[j] for j in odd]), axis, bit)
+        for k, j in enumerate(even):
+            parts[j] = add_low(parts[j], moved[k])
+        bit *= 2
+    return parts[0]
+
+
+def add_low(left, right):
+    return (left.astype(jnp.float32) + right.astype(jnp.float32)).astype(left.dtype)
+
+
+def ring_order(size):
+    return list(range(0, 1)) + list(range(1, size, 2)) + list(range(size - 2, 0, -2))
+
+
+def relative_index(axis):
+    size = lax.axis_size(axis)
+    high = size // 2
+    order = jnp.asarray(ring_order(high), jnp.int32)
+    place = [ring_order(high).index(i) for i in range(high)]
+    me = lax.axis_index(axis)
+    mine = jnp.asarray(place, jnp.int32)[me // 2]
+    steps = jnp.mod(mine - 1 - jnp.arange(high, dtype=jnp.int32), high)
+    lows = me % 2
+    return jnp.stack([order[steps] * 2 + (lows ^ low) for low in range(2)]).reshape(size)
+
+
+def ring_scatter(parts, axis, pair_first):
+    high = parts.shape[1]
+    order = ring_order(high)
+    links = [
+        (order[k] * 2 + low, order[(k + 1) % high] * 2 + low) for k in range(high) for low in range(2)
+    ]
+
+    def ring(value):
+        total = value[0]
+        for step in range(high - 1):
+            total = add_low(lax.ppermute(total, axis, links), value[step + 1])
+        return total
+
+    if pair_first:
+        return ring(add_low(parts[0], swap(parts[1], axis, 1)))
+    total = ring(parts.transpose((1, 0) + tuple(range(2, parts.ndim))))
+    return add_low(total[0], swap(total[1], axis, 1))
+
+
+def pick_parts(value, index):
+    count = value.shape[0]
+    parts = [lax.dynamic_index_in_dim(value, index[k], 0, keepdims=False) for k in range(count)]
+    return jnp.stack(parts).reshape((2, count // 2) + value.shape[1:])
+
+
+def stats_kernel(cols, steps, embed_ref, z_ref, out_ref, max_ref, sum_ref, mix_ref):
+    step = pl.program_id(0)
+    half = z_ref.shape[0] // 2
+
+    @pl.when(step == 0)
+    def _():
+        max_ref[...] = jnp.full_like(max_ref, -jnp.inf)
+        sum_ref[...] = jnp.zeros_like(sum_ref)
+        mix_ref[...] = jnp.zeros_like(mix_ref)
+
+    embed = embed_ref[...]
+    for col in range(half // cols):
+        places = [slice(p * half + col * cols, p * half + (col + 1) * cols) for p in range(2)]
+        logits = [dot(embed, z_ref[place, :], NT).reshape(-1, 8, cols) for place in places]
+        apart = logits[0] - logits[1]
+        for place, logit in zip(places, logits):
+            old = max_ref[:, place]
+            new = jnp.maximum(old, jnp.max(logit, axis=0))
+            max_ref[:, place] = new
+            scale = jnp.exp2((old - new) * LOG2E)
+            weights = jnp.exp2((logit - new[None]) * LOG2E)
+            sum_ref[:, place] = sum_ref[:, place] * scale + jnp.sum(weights, axis=0)
+            mix_ref[:, place] = mix_ref[:, place] * scale + jnp.sum(weights * apart, axis=0)
+
+    @pl.when(step == steps - 1)
+    def _():
+        top = jnp.max(max_ref[...], axis=0, keepdims=True)
+        scale = jnp.exp2((max_ref[...] - top) * LOG2E)
+        out_ref[0:1, :] = top
+        out_ref[1:2, :] = jnp.sum(sum_ref[...] * scale, axis=0, keepdims=True)
+        out_ref[2:3, :] = jnp.sum(mix_ref[...] * scale, axis=0, keepdims=True)
+
+
+def row_tile(rows, limit):
+    return max(size for size in range(16, limit + 1, 16) if rows % size == 0)
+
+
+def vocab_stats(embed, z_rows):
+    vocab, width = embed.shape
+    rows = z_rows.shape[0]
+    tile = row_tile(vocab, 800)
+    cols = min(256, rows // 2)
+    steps = vocab // tile
+    return pl.pallas_call(
+        functools.partial(stats_kernel, cols, steps),
+        grid=(steps,),
+        in_specs=[
+            pl.BlockSpec((tile, width), lambda i: (i, 0)),
+            pl.BlockSpec((rows, width), lambda i: (0, 0)),
+        ],
+        out_specs=pl.BlockSpec((3, rows), lambda i: (0, 0)),
+        out_shape=jax.ShapeDtypeStruct((3, rows), jnp.float32),
+        scratch_shapes=[pltpu.VMEM((8, rows), jnp.float32)] * 3,
+        compiler_params=pltpu.CompilerParams(vmem_limit_bytes=48 << 20),
+        cost_estimate=pl.CostEstimate(
+            flops=2 * vocab * rows * width,
+            bytes_accessed=2 * (vocab + rows) * width,
+            transcendentals=vocab * rows,
+        ),
+    )(embed, z_rows)
+
+
+def loss_back_kernel(cols, steps, has_total, has_carry, last, *refs):
+    base_ref, embed_ref, embed_t_ref, z_ref, z_t_ref, row_ref, label_ref = refs[:7]
+    refs = list(refs[7:])
+    total_ref = refs.pop(0) if has_total else None
+    carry_ref = refs.pop(0) if has_carry else None
+    grad_embed_ref, grad_z_ref, loss_ref, grad_ref, sum_ref = refs
+    step = pl.program_id(0)
+    half = z_ref.shape[0] // 2
+    tile = embed_ref.shape[0]
+
+    @pl.when(step == 0)
+    def _():
+        sum_ref[...] = carry_ref[...] if has_carry else jnp.zeros_like(sum_ref)
+        loss_ref[...] = jnp.zeros_like(loss_ref)
+
+    embed = embed_ref[...]
+    ids = lax.broadcasted_iota(jnp.int32, (tile // 8, 8, cols), 0) * 8
+    ids = ids + lax.broadcasted_iota(jnp.int32, (tile // 8, 8, cols), 1)
+    base = base_ref[0] + step * tile
+    for col in range(half // cols):
+        one = slice(col * cols, (col + 1) * cols)
+        two = slice(half + col * cols, half + (col + 1) * cols)
+        logit_one = dot(embed, z_ref[one, :], NT).reshape(-1, 8, cols)
+        logit_two = dot(embed, z_ref[two, :], NT).reshape(-1, 8, cols)
+        row = [row_ref[k : k + 1, one].reshape(1, 1, cols) for k in range(6)]
+        prob_one = jnp.exp2(logit_one * LOG2E - row[0])
+        prob_two = jnp.exp2(logit_two * LOG2E - row[1])
+        apart = logit_one - logit_two
+        hits = ids == (label_ref[0:1, one] - base).reshape(1, 1, cols)
+        smooth = jnp.where(hits, row[4], row[5])
+        grad_one = prob_one * (apart + row[2]) - (prob_two + smooth)
+        grad_two = prob_two * (row[3] - apart) - (prob_one + smooth)
+        loss_ref[:, one] += jnp.sum(smooth * (logit_one + logit_two), axis=0)
+        grad_ref[:, one] = grad_one.reshape(tile, cols).astype(jnp.bfloat16)
+        grad_ref[:, two] = grad_two.reshape(tile, cols).astype(jnp.bfloat16)
+    grads = grad_ref[...]
+    grad_embed = dot(z_t_ref[...], grads, NT)
+    if has_total:
+        grad_embed = grad_embed + total_ref[...]
+    grad_embed_ref[...] = grad_embed.astype(grad_embed_ref.dtype)
+    sum_ref[...] += dot(embed_t_ref[...], grads, NN)
+
+    @pl.when(step == steps - 1)
+    def _():
+        if last:
+            grad_z_ref[...] = sum_ref[...].T.astype(grad_z_ref.dtype)
+        else:
+            grad_z_ref[...] = sum_ref[...]
+
+
+def loss_back(base, embed, embed_t, z_rows, z_t, row_values, labels, span, total, carry, last):
+    width = embed.shape[1]
+    rows = z_rows.shape[0]
+    tile = TILE
+    low, high = span
+    steps, first = (high - low) // tile, low // tile
+    cols = min(256, rows // 2)
+    operands = [base + low, embed, embed_t, z_rows, z_t, row_values, labels]
+    whole = lambda i: (0, 0)
+    specs = [
+        pl.BlockSpec(memory_space=pltpu.SMEM),
+        pl.BlockSpec((tile, width), lambda i: (i + first, 0)),
+        pl.BlockSpec((width, tile), lambda i: (0, i + first)),
+        pl.BlockSpec((rows, width), whole),
+        pl.BlockSpec((width, rows), whole),
+        pl.BlockSpec((6, rows // 2), whole),
+        pl.BlockSpec((1, rows // 2), whole),
+    ]
+    if total is not None:
+        operands.append(total)
+        specs.append(pl.BlockSpec((width, tile), lambda i: (0, i + first)))
+    if carry is not None:
+        operands.append(carry)
+        specs.append(pl.BlockSpec((width, rows), whole))
+    emit = jnp.bfloat16 if last is not None else jnp.float32
+    grad_z = (
+        jax.ShapeDtypeStruct((rows, width), jnp.bfloat16)
+        if last is not False
+        else jax.ShapeDtypeStruct((width, rows), jnp.float32)
+    )
+    return pl.pallas_call(
+        functools.partial(
+            loss_back_kernel, cols, steps, total is not None, carry is not None, last is not False
+        ),
+        grid=(steps,),
+        in_specs=specs,
+        out_specs=[
+            pl.BlockSpec((width, tile), lambda i: (0, i)),
+            pl.BlockSpec(grad_z.shape, whole),
+            pl.BlockSpec((8, rows // 2), whole),
+        ],
+        out_shape=[
+            jax.ShapeDtypeStruct((width, high - low), emit),
+            grad_z,
+            jax.ShapeDtypeStruct((8, rows // 2), jnp.float32),
+        ],
+        scratch_shapes=[
+            pltpu.VMEM((tile, rows), jnp.bfloat16),
+            pltpu.VMEM((width, rows), jnp.float32),
+        ],
+        compiler_params=pltpu.CompilerParams(vmem_limit_bytes=56 << 20),
+        cost_estimate=pl.CostEstimate(
+            flops=6 * (high - low) * rows * width,
+            bytes_accessed=8 * (high - low) * width,
+            transcendentals=(high - low) * rows,
+        ),
+    )(*operands)
+
+
+TILE = 1024
+
+
+def join_stats(first, second):
+    top = jnp.maximum(first[0], second[0])
+    scale_one, scale_two = jnp.exp(first[0] - top), jnp.exp(second[0] - top)
+    return jnp.stack(
+        [top, first[1] * scale_one + second[1] * scale_two, first[2] * scale_one + second[2] * scale_two]
+    )
 
 
 def norm_rows(values, gain):
@@ -211,87 +473,92 @@
     )
     outputs = after_cross[None] + expert_out
     z_pair = norm_rows(outputs, gain_out).astype(jnp.bfloat16)
-    group_z = lax.all_gather(z_pair, "blk", axis=1, tiled=True)
-    seq_len = group_z.shape[1]
+    z_blocks = gather_blocks(z_pair, "blk")
     vocab_part = embed.shape[0]
     vocab_total = vocab_part * group_size
-    vocab_ids = group_index * vocab_part + jnp.arange(vocab_part, dtype=jnp.int32)
-    block = min(1024, seq_len)
-    steps_count = seq_len // block
-    z_blocks = group_z.reshape(2, steps_count, block, model_width).transpose(1, 0, 2, 3)
-    labels = targets[0].reshape(steps_count, block)
-
-    def partial_stats(operands):
-        z_block, label_block = operands
-        logit_pair = jnp.einsum("prd,vd->prv", z_block, embed, preferred_element_type=jnp.float32)
-        difference = logit_pair[0] - logit_pair[1]
-        row_max = jnp.max(logit_pair, axis=-1)
-        weights = jnp.exp(logit_pair - row_max[..., None])
-        row_total = jnp.sum(weights, axis=-1)
-        weighted = jnp.sum(weights * difference[None], axis=-1)
-        hits = (label_block[:, None] == vocab_ids[None, :]).astype(jnp.float32)
-        picked = jnp.sum(logit_pair * hits[None], axis=-1)
-        summed = jnp.sum(logit_pair, axis=-1)
-        return (row_max, row_total, weighted, picked, summed)
-
-    stats = lax.map(partial_stats, (z_blocks, labels))
-
-    def join(first, second):
-        max_one, total_one, weight_one, pick_one, sum_one = first
-        max_two, total_two, weight_two, pick_two, sum_two = second
-        joined_max = jnp.maximum(max_one, max_two)
-        scale_one = jnp.exp(max_one - joined_max)
-        scale_two = jnp.exp(max_two - joined_max)
-        return (
-            joined_max,
-            total_one * scale_one + total_two * scale_two,
-            weight_one * scale_one + weight_two * scale_two,
-            pick_one + pick_two,
-            sum_one + sum_two,
-        )
-
-    row_max, row_total, weighted, picked, summed = combined_all(stats, "blk", join)
-    log_total = row_max + jnp.log(row_total)
-    expect = weighted / row_total
-    cross_entropy = log_total - (1.0 - SMOOTH) * picked - SMOOTH * summed / vocab_total
-    live = (
-        (jnp.arange(seq_len, dtype=jnp.int32) < lengths[0])
-        .astype(jnp.float32)
-        .reshape(steps_count, block)
-    )
-    losses = (
-        live * (cross_entropy[:, 0] + cross_entropy[:, 1] + expect[:, 0] - expect[:, 1])
-    ).reshape(seq_len)
-    own_loss = lax.dynamic_slice_in_dim(losses, group_index * own_rows, own_rows)
-
-    def grad_block(carry, operands):
-        z_block, label_block, lse_block, expect_block, live_block = operands
-        logit_pair = jnp.einsum("prd,vd->prv", z_block, embed, preferred_element_type=jnp.float32)
-        probs = jnp.exp(logit_pair - lse_block[..., None])
-        difference = logit_pair[0] - logit_pair[1]
-        hits = (label_block[:, None] == vocab_ids[None, :]).astype(jnp.float32)
-        smooth = (1.0 - SMOOTH) * hits + SMOOTH / vocab_total
-        apart = probs[0] - probs[1]
-        grad_zero = probs[0] - smooth + apart + probs[0] * (difference - expect_block[0][:, None])
-        grad_one = probs[1] - smooth - apart - probs[1] * (difference - expect_block[1][:, None])
-        grad_logits = (jnp.stack([grad_zero, grad_one]) * live_block[None, :, None]).astype(
-            jnp.bfloat16
-        )
-        grad_z = jnp.einsum("prv,vd->prd", grad_logits, embed, preferred_element_type=jnp.float32)
-        carry = carry + jnp.einsum(
-            "prv,prd->vd", grad_logits, z_block, preferred_element_type=jnp.float32
-        )
-        return (carry, grad_z)
-
-    embed_local, grad_z_blocks = lax.scan(
-        grad_block,
-        jnp.zeros((vocab_part, model_width), jnp.float32),
-        (z_blocks, labels, log_total, expect, live),
-    )
-    grad_z_group = grad_z_blocks.transpose(1, 0, 2, 3).reshape(2, seq_len, model_width)
-    grad_z_own = lax.psum_scatter(
-        grad_z_group.astype(jnp.bfloat16), "blk", scatter_dimension=1, tiled=True
+    padded = -(-vocab_part // TILE) * TILE
+    embed_pad = jnp.pad(embed, ((0, padded - vocab_part), (0, 0)))
+    embed_t = embed_pad.T
+    count = max(2, group_size * own_rows // 1024)
+    per_group = group_size // count
+    groups = [list(range(k * per_group, (k + 1) * per_group)) for k in range(count)]
+    group_z = [
+        jnp.stack([z_blocks[j] for j in group], axis=1).reshape(-1, model_width) for group in groups
+    ]
+    stats = jnp.stack([vocab_stats(embed, rows) for rows in group_z])
+    stats = stats.reshape(count, 3, 2, per_group, own_rows).transpose(1, 0, 3, 2, 4)
+    stats = stats.reshape(3, group_size, 2, own_rows)
+    bit = 1
+    while bit < group_size:
+        moved = swap(stats, "blk", bit)
+        moved = moved.reshape(3, group_size // (2 * bit), 2, bit, 2, own_rows)[:, :, ::-1]
+        stats = join_stats(stats, moved.reshape(stats.shape))
+        bit *= 2
+    log_total = stats[0] + jnp.log(stats[1])
+    expect = stats[2] / stats[1]
+    positions = jnp.stack(
+        [
+            (group_index ^ j) * own_rows + jnp.arange(own_rows, dtype=jnp.int32)
+            for j in range(group_size)
+        ]
+    )
+    live = positions < lengths[0]
+    labels = jnp.stack(
+        [
+            lax.dynamic_slice_in_dim(targets[0], (group_index ^ j) * own_rows, own_rows)
+            for j in range(group_size)
+        ]
+    )
+    labels = jnp.where(live, labels, -1)
+    live = live.astype(jnp.float32)
+    row_values = jnp.stack(
+        [
+            jnp.where(live > 0, log_total[:, 0] * LOG2E, 1e30),
+            jnp.where(live > 0, log_total[:, 1] * LOG2E, 1e30),
+            2.0 - expect[:, 0],
+            2.0 + expect[:, 1],
+            live * (1.0 - SMOOTH + SMOOTH / vocab_total),
+            live * (SMOOTH / vocab_total),
+        ]
+    )
+    relative = relative_index("batch")
+    vocab_base = (group_index * vocab_part).astype(jnp.int32).reshape(1)
+    total = None
+    grad_z_parts, smooth_parts, embed_chunks = {}, {}, []
+    for at in range(count - 1, -1, -1):
+        group = groups[at]
+        z_t = group_z[at].T
+        z_t = pick_parts(z_t.reshape(batch_size, -1, z_t.shape[1]), relative).reshape(z_t.shape)
+        at_rows = [group[0], group[-1] + 1]
+        part_rows = row_values[:, at_rows[0] : at_rows[1]].reshape(6, -1)
+        part_labels = labels[at_rows[0] : at_rows[1]].reshape(1, -1)
+        if at > 0:
+            total, grad_z, smooth = loss_back(
+                vocab_base, embed_pad, embed_t, group_z[at], z_t, part_rows, part_labels,
+                (0, padded), total, None, None,
+            )
+        else:
+            grad_z, smooth = None, 0.0
+            chunk = max(padded // 4, TILE)
+            for low in range(0, padded, chunk):
+                grad_embed, grad_z, more = loss_back(
+                    vocab_base, embed_pad, embed_t, group_z[at], z_t, part_rows, part_labels,
+                    (low, low + chunk), total, grad_z, low + chunk == padded,
+                )
+                smooth = smooth + more
+                grad_embed = grad_embed.reshape(2, batch_size // 2, model_width // batch_size, chunk)
+                embed_chunks.append(ring_scatter(grad_embed, "batch", low > 0))
+        grad_z = grad_z.reshape(2, per_group, own_rows, model_width)
+        smooth = jnp.sum(smooth, axis=0).reshape(per_group, own_rows)
+        for k, j in enumerate(group):
+            grad_z_parts[j] = grad_z[:, k]
+            smooth_parts[j] = smooth[k]
+    grad_z_own = scatter_blocks(
+        [grad_z_parts[j] for j in range(group_size)], "blk"
     ).astype(jnp.float32)
+    smooth_own = scatter_blocks([smooth_parts[j] for j in range(group_size)], "blk")
+    own_loss = live[0] * (log_total[0, 0] + log_total[0, 1] + expect[0, 0] - expect[0, 1]) - smooth_own
+    embed_sum = jnp.concatenate(embed_chunks, axis=-1)[:, :vocab_part].astype(jnp.float32).T
     grad_outputs, grad_gain_out = norm_back(outputs, gain_out, grad_z_own)
     send_grads = jnp.einsum(
         "psr,prd->psd",
@@ -377,31 +644,32 @@
     grad_h_one = grad_h_one + own_key_term
     norm_part, grad_gain_self = norm_back(own_states, gain_self, grad_h_one)
     grad_tokens = grad_middle + norm_part
-    stacked_weights = jnp.stack(
-        [grad_wq, grad_wk, grad_wv, grad_wo, grad_cq, grad_ck, grad_cv, grad_co]
-    )
     row_part = model_width // batch_size
     col_part = model_width // group_size
-    tiled = (
-        stacked_weights.reshape(8, batch_size, row_part, group_size, col_part)
-        .transpose(0, 1, 3, 2, 4)
-        .reshape(8, model_width * model_width)
-    )
-    summed_flat = lax.psum_scatter(tiled, ("batch", "blk"), scatter_dimension=1, tiled=True)
-    summed_weights = summed_flat.reshape(8, row_part, col_part)
-    stacked_gains = jnp.stack([grad_gain_self, grad_gain_cross, grad_gain_ffn, grad_gain_out])
-    summed_gains = lax.psum(stacked_gains, ("batch", "blk"))
-    w_in_sum, w_out_sum, embed_sum = (
-        lax.psum_scatter(
-            w_in_local.astype(jnp.bfloat16), "batch", scatter_dimension=1, tiled=True
-        ).astype(jnp.float32),
-        lax.psum_scatter(
-            w_out_local.astype(jnp.bfloat16), "batch", scatter_dimension=1, tiled=True
-        ).astype(jnp.float32),
-        lax.psum_scatter(
-            embed_local.astype(jnp.bfloat16), "batch", scatter_dimension=1, tiled=True
-        ).astype(jnp.float32),
-    )
+
+    def sum_weights(weights):
+        stacked = jnp.stack([weight.astype(jnp.bfloat16) for weight in weights])
+        parts = [
+            lax.dynamic_slice_in_dim(stacked, (group_index ^ j) * col_part, col_part, axis=2)
+            for j in range(group_size)
+        ]
+        summed = scatter_blocks(parts, "blk")
+        summed = summed.reshape(len(weights), batch_size, row_part, col_part).transpose(1, 0, 2, 3)
+        return ring_scatter(pick_parts(summed, relative), "batch", True).astype(jnp.float32)
+
+    cross_sums = sum_weights([grad_cq, grad_ck, grad_cv, grad_co])
+    self_sums = sum_weights([grad_wq, grad_wk, grad_wv, grad_wo])
+    summed_weights = [self_sums[k] for k in range(4)] + [cross_sums[k] for k in range(4)]
+    summed_gains = jnp.stack([grad_gain_self, grad_gain_cross, grad_gain_ffn, grad_gain_out])
+    for axis in ("blk", "batch"):
+        bit = 1
+        while bit < lax.axis_size(axis):
+            summed_gains = summed_gains + swap(summed_gains, axis, bit)
+            bit *= 2
+    w_in_parts = w_in_local[0].astype(jnp.bfloat16).reshape(batch_size, row_part, -1)
+    w_in_sum = ring_scatter(pick_parts(w_in_parts, relative), "batch", True).astype(jnp.float32)[None]
+    w_out_parts = w_out_local[0].astype(jnp.bfloat16).reshape(batch_size, -1, model_width)
+    w_out_sum = ring_scatter(pick_parts(w_out_parts, relative), "batch", True).astype(jnp.float32)[None]
     return (
         own_loss[None],
         grad_tokens[None],

time: 1260 us -> 778 us (0.62)
  waiting for transfers between devices: 475 us -> 128 us
  other arithmetic: 227 us -> 58.1 us
  Pallas kernels: 0 us -> 128 us
  blocking collectives: 109 us -> 0 us
  matrix products: 326 us -> 221 us
  starting transfers between devices: 4.53 us -> 63.3 us
  local copies, waits for them, and re-layouts: 85 us -> 132 us
  between operations: 16.1 us -> 32.9 us
    reduce_scatter x5 -> x0, waiting for transfers between devices: 392 us -> none  [the longest x1 148 us: per_device(): lax.psum_scatter(embed_local.astype(jnp.bfloat16), 'batch', scatter_dimen...]
    pallas_call x0 -> x7, Pallas kernels: none -> 128 us  [the longest x5 91 us: loss_back(): pl.pallas_call(functools.partial(loss_back_kernel, cols, steps, total is...]
    ppermute x0 -> x50, waiting for transfers between devices: none -> 99 us  [the longest x24 63.2 us: ring(): total = add_low(lax.ppermute(total, axis, links), value[step + 1])]
    dot_general x3 -> x0, matrix products: 89.3 us -> none  [the longest x1 30.3 us: partial_stats(): jnp.einsum('prd,vd->prv', z_block, embed, preferred_element_type=jnp.floa...]
    add x27 -> x29, other arithmetic: 63.2 us -> 0.37 us  [the longest x1 0.12 us: per_device(): grad_after = grad_outputs[0] + grad_outputs[1] + norm_part]
    ppermute x0 -> x50, starting transfers between devices: none -> 47.9 us  [the longest x24 29.1 us: ring(): total = add_low(lax.ppermute(total, axis, links), value[step + 1])]
    exp x1 -> x0, other arithmetic: 43.4 us -> none  [grad_block(): probs = jnp.exp(logit_pair - lse_block[..., None])]
    all_to_all x3 -> x0, blocking collectives: 42.6 us -> none  [the longest x1 14.3 us: per_device(): lax.all_to_all(result, 'blk', split_axis=1, concat_axis=1, tiled=True)]
  transfers between devices with their start and end apart: 15 -> 62, of which waited for: 10 -> 34; matrix products, arithmetic and copies ran while one was open for 14% -> 44% of each run, Pallas kernels for 0% -> 8%
where the time goes in v1:
time: 778 us; the launch traced here: 764 us
  matrix products  221 us (28%)
  local copies, waits for them, and re-layouts  132 us (17%)
  waiting for transfers between devices  128 us (16%)
  Pallas kernels  128 us (16%)
  starting transfers between devices  63.3 us (8%)
  other arithmetic  58.1 us (7%)
  between operations  32.9 us (4%)
    pallas_call x5, Pallas kernels, loss_back(): pl.pallas_call(functools.partial(loss_back_kernel, cols, steps, total is...  91 us
    ppermute x24, waiting for transfers between devices, ring(): total = add_low(lax.ppermute(total, axis, links), value[step + 1])  63.2 us
    unnamed x234, local copies, waits for them, and re-layouts  49.9 us
    dot_general x32, matrix products, head_scores(): jnp.einsum('qd,kd->qk', query_head, key_head, preferred_element_type=jnp....  46.5 us
    pallas_call x2, Pallas kernels, vocab_stats(): pl.pallas_call(functools.partial(stats_kernel, cols, steps), grid=(steps,...  36.8 us
    ppermute x26, waiting for transfers between devices, swap(): return lax.ppermute(value, axis, [(i, i ^ mask) for i in range(size)])  35.9 us
    ppermute x24, starting transfers between devices, ring(): total = add_low(lax.ppermute(total, axis, links), value[step + 1])  29.1 us
    dot_general x16, matrix products, one_head(): jnp.dot(probs, value_head, preferred_element_type=jnp.float32)  26.4 us
  transfers between devices with their start and end apart: 62, of which 34 were waited for; matrix products, arithmetic and copies ran while one was open for 44% of the time, Pallas kernels for 8%

profile of v1, /device:TPU:0, one launch (start us, length us, event | category | flops | bytes accessed | tf_op | source)
XLA Modules:
  0.0 764.4 jit_solution(17552287937287194603)
XLA Ops:
  23.6 11.7 %copy.235 = bf16[8000,512]{0,1:T(8,128)(2,1)} copy(bf16[8000,512]{1,0:T(8,128)(2,1)} %embed_ref.3) | data formatting | bytes 16384000 | tf_op args[19]
  38.6 12.5 %all-gather.7.cloned.1.call-done = bf16[1024,512]{1,0:T(8,128)(2,1)} async-done(((bf16[256,512]{1,0:T(8,128)(2,1)}), bf16[1024,512]{1,0:T(8,128)(2,1)}) %all-gather.7.cloned.1.call-update) | async-done | bytes 1048592 | tf_op jit(solution)/shard_map/all_gather | solution.py:428
  55.1 29.8 %while.56 = (s32[]{:T(128)}, bf16[8,256,64]{1,2,0:T(8,128)(2,1)}, f32[8,256]{1,0:T(8,128)S(1)}, bf16[8,256,64]{2,1,0:T(8,128)(2,1)}, bf16[8,1024,64]{2,1,0:T(8,1...) while((s32[]{:T(128)}, bf16[8,256,64]{1,2,0:T(8,128)(2,1)}, ...), condition=%wide.region_5.6_spmd.clone, body=%wide.region_2.5_spmd.clone.sunk | while | flops 69484544 | bytes 3782757 | solution.py:335
  95.5 24.9 %while.54 = (s32[]{:T(128)}, bf16[8,256,64]{1,2,0:T(8,128)(2,1)S(1)}, f32[8,256]{1,0:T(8,128)S(1)}, bf16[8,256,64]{2,1,0:T(8,128)(2,1)}, bf16[8,1024,64]{2,1,0:T...) while((s32[]{:T(128)}, bf16[8,256,64]{1,2,0:T(8,128)(2,1)S(1)}, ...), condition=%wide.region_11.12_spmd, body=%wide.region_8.11_spmd.sunk | while | flops 68960000 | bytes 3780697 | solution.py:335
  124.5 4.0 all-to-all-start
  128.4 7.9 %pad_bitcast_fusion.refs_2_ = bf16[512,8192]{1,0:T(8,128)(2,1)} fusion(bf16[8000,512]{0,1:T(8,128)(2,1)} %copy.235), kind=kLoop, calls=%fused_computation.567 | loop fusion | bytes 16580608 | tf_op jit(solution)/shard_map/transpose | solution.py:481
  140.1 4.3 fusion.98
  148.0 3.5 all-to-all-start.1
  152.4 10.8 %all-to-all-done.1 = bf16[2,4,96,512]{3,2,0,1:T(8,128)(2,1)S(1)} async-done(((bf16[2,4,96,512]{3,2,0,1:T(8,128)(2,1)}), bf16[2,4,96,512]{3,2,0,1:T(8,128)(2,1)S(1)}, u32[]{:S(2)}, u32[]{:S(2)}) %all-to-all-start.1) | async-done | bytes 786464 | tf_op jit(solution)/shard_map/all_to_all | solution.py:466
  177.3 11.7 %copy.396 = bf16[8000,512]{1,0:T(8,128)(2,1)} copy(bf16[8000,512]{0,1:T(8,128)(2,1)} %copy.235) | data formatting | bytes 16384000
  195.2 7.1 pad.4.clone.refs_1_
  202.3 4.6 copy.274
  211.0 18.4 %shard_map.349 = f32[3,1024]{1,0:T(4,128)S(1)} custom-call(bf16[8000,512]{1,0:T(8,128)(2,1)} %embed_ref.3, bf16[1024,512]{1,0:T(8,128)(2,1)S(1)} %bitcast.831), custom_call_target="tpu_custom_call" | custom-call | flops 8388608000 | bytes 9240576 | tf_op jit(solution)/shard_map/pallas_call | solution.py:145
  233.6 18.4 %shard_map.350 = f32[3,1024]{1,0:T(4,128)S(1)} custom-call(bf16[8000,512]{1,0:T(8,128)(2,1)} %embed_ref.3, bf16[1024,512]{1,0:T(8,128)(2,1)S(1)} %bitcast.838), custom_call_target="tpu_custom_call" | custom-call | flops 8388608000 | bytes 9240576 | tf_op jit(solution)/shard_map/pallas_call | solution.py:145
  268.0 36.0 %shard_map.351 = (f32[512,8192]{1,0:T(8,128)}, bf16[1024,512]{1,0:T(8,128)(2,1)}, f32[8,512]{1,0:T(8,128)}) custom-call(s32[1]{0:T(128)} %bitcast.72.refs_0_, bf16[8192,512]{1,0:T(8,128)(2,1)} %pad.4.clone.refs_1_, bf16[512,8192]{1,0:T(8,128)(2,1)} %pad_bitcast_fusion.refs_2_, bf16[1024,512]{1,0:T(8,128)(2,1)} %bitcast.839, bf16[512,1024]{1,0:T(8,128)(2,1)} %bitcast.958, ...), custom_call_target="tpu_custom_call" | custom-call | flops 25769803776 | bytes 33554432 | tf_op jit(solution)/shard_map/pallas_call | solution.py:244
  304.0 13.4 %shard_map.352 = (bf16[512,2048]{1,0:T(8,128)(2,1)}, f32[512,1024]{1,0:T(8,128)}, f32[8,512]{1,0:T(8,128)}) custom-call(s32[1]{0:T(128)} %bitcast.72.refs_0_, bf16[8192,512]{1,0:T(8,128)(2,1)} %pad.4.clone.refs_1_, bf16[512,8192]{1,0:T(8,128)(2,1)} %pad_bitcast_fusion.refs_2_, bf16[1024,512]{1,0:T(8,128)(2,1)} %bitcast.833, bf16[512,1024]{1,0:T(8,128)(2,1)} %bitcast.840, ...), custom_call_target="tpu_custom_call" | custom-call | flops 6442450944 | bytes 8388608 | tf_op jit(solution)/shard_map/pallas_call | solution.py:244
  322.8 13.8 %shard_map.353 = (bf16[512,2048]{1,0:T(8,128)(2,1)}, f32[512,1024]{1,0:T(8,128)}, f32[8,512]{1,0:T(8,128)}) custom-call(s32[1]{0:T(128)S(6)} %add.695.refs_0_, bf16[8192,512]{1,0:T(8,128)(2,1)} %pad.4.clone.refs_1_, bf16[512,8192]{1,0:T(8,128)(2,1)} %pad_bitcast_fusion.refs_2_, bf16[1024,512]{1,0:T(8,128)(2,1)} %bitcast.834, bf16[512,1024]{1,0:T(8,128)(2,1)} %bitcast.841, ...), custom_call_target="tpu_custom_call" | custom-call | flops 6442450944 | bytes 8388608 | tf_op jit(solution)/shard_map/pallas_call | solution.py:244
  336.6 3.1 fusion.260
  341.2 13.9 %shard_map.354 = (bf16[512,2048]{1,0:T(8,128)(2,1)}, f32[512,1024]{1,0:T(8,128)}, f32[8,512]{1,0:T(8,128)}) custom-call(s32[1]{0:T(128)S(6)} %add.697.refs_0_, bf16[8192,512]{1,0:T(8,128)(2,1)} %pad.4.clone.refs_1_, bf16[512,8192]{1,0:T(8,128)(2,1)} %pad_bitcast_fusion.refs_2_, bf16[1024,512]{1,0:T(8,128)(2,1)} %bitcast.835, bf16[512,1024]{1,0:T(8,128)(2,1)} %bitcast.842, ...), custom_call_target="tpu_custom_call" | custom-call | flops 6442450944 | bytes 8388608 | tf_op jit(solution)/shard_map/pallas_call | solution.py:244
  355.1 3.1 fusion.261
  358.8 13.9 %shard_map.355 = (bf16[512,2048]{1,0:T(8,128)(2,1)}, bf16[1024,512]{1,0:T(8,128)(2,1)}, f32[8,512]{1,0:T(8,128)}) custom-call(s32[1]{0:T(128)S(6)} %add.699.refs_0_, bf16[8192,512]{1,0:T(8,128)(2,1)} %pad.4.clone.refs_1_, bf16[512,8192]{1,0:T(8,128)(2,1)} %pad_bitcast_fusion.refs_2_, bf16[1024,512]{1,0:T(8,128)(2,1)} %bitcast.836, ...), custom_call_target="tpu_custom_call" | custom-call | flops 6442450944 | bytes 8388608 | tf_op jit(solution)/shard_map/pallas_call | solution.py:244
  372.8 3.2 fusion.262
  387.8 8.5 %collective-permute-done.35 = bf16[2,64,2048]{2,1,0:T(8,128)(2,1)S(1)} collective-permute-done((bf16[2,64,2048]{2,1,0:T(8,128)(2,1)S(1)}, bf16[2,64,2048]{2,1,0:T(8,128)(2,1)S(1)}, u32[]{:S(2)}, u32[]{:S(2)}) %collective-permute-start.35) | collective-permute-done | bytes 524320 | tf_op jit(solution)/shard_map/ppermute | solution.py:87
  404.0 5.2 collective-permute-done.46
  415.0 2.8 collective-permute-done.39
  418.6 4.8 collective-permute-done.43
  424.9 4.2 collective-permute-done.47
  436.0 4.2 all-to-all-start.2
  451.4 5.5 collective-permute-done.45
  458.0 4.1 collective-permute-done.49
  465.8 8.1 %fusion.90 = bf16[768,2048]{1,0:T(8,128)(2,1)S(1)} fusion(f32[768,2048]{1,0:T(8,128)} %copy-done.103, bf16[768,512]{1,0:T(8,128)(2,1)S(1)} %bitcast.901, bf16[1,2048,512]{2,1,0:T(8,128)(2,1)} %param.48), kind=kOutput, calls=%fused_computation.120 | convolution fusion | flops 1642070016 | bytes 12320768 | tf_op jit(solution)/shard_map/erd,efd->erf/dot_general | solution.py:575
  476.7 3.5 all-to-all-start.3
  480.2 3.9 convolution_convert_fusion.2
  487.8 4.1 all-to-all-done.3
  496.5 61.0 %while.55 = (s32[]{:T(128)}, bf16[8,256,64]{1,2,0:T(8,128)(2,1)S(1)}, bf16[8,1024,64]{1,2,0:T(8,128)(2,1)S(1)}, bf16[8,1024,64]{1,2,0:T(8,128)(2,1)}, bf16[8,256...) while((s32[]{:T(128)}, ...), condition=%wide.region_27.28_spmd, body=%wide.region_25.27_spmd.sunk | while | flops 169950976 | bytes 9447529 | solution.py:370
  558.6 3.9 fusion.102
  570.9 67.2 %while.57 = (s32[]{:T(128)}, bf16[8,256,64]{1,2,0:T(8,128)(2,1)S(1)}, bf16[8,1024,64]{1,2,0:T(8,128)(2,1)}, bf16[8,1024,64]{1,2,0:T(8,128)(2,1)}, bf16[8,256,64]...) while((s32[]{:T(128)}, ...), condition=%wide.region_32.33_spmd.clone, body=%wide.region_30.32_spmd.clone.sunk | while | flops 170475520 | bytes 9449589 | solution.py:370
  650.2 4.6 collective-permute-done.31
  656.1 4.3 collective-permute-done.27
  662.9 3.3 collective-permute-done.32
  667.9 3.9 collective-permute-done.28
  674.6 2.8 collective-permute-done.33
  699.5 3.0 collective-permute-done.10
  707.2 2.7 collective-permute-done.12
  716.0 10.9 %collective-permute-done.21 = bf16[1,4,512,128]{3,2,1,0:T(8,128)(2,1)S(1)} collective-permute-done((bf16[1,4,512,128]{3,2,1,0:T(8,128)(2,1)S(1)}, bf16[1,4,512,128]{3,2,1,0:T(8,128)(2,1)S(1)}, u32[]{:S(2)}, u32[]{:S(2)}) %collective-permute-start.21) | collective-permute-done | bytes 524320 | tf_op jit(solution)/shard_map/ppermute | solution.py:27
  728.8 5.1 collective-permute-done.15
  736.5 2.7 collective-permute-start.23
  754.1 2.6 collective-permute-done.19
  (775 shorter events, 406.4 us)
Async XLA Ops:
  7.2 28.1 %all-gather.5.cloned.1.call-start = ((), (), s32[]{:S(2)}) async-start(), calls=%async_computation.8 | async-start | bytes 1310720 | tf_op jit(solution)/shard_map/all_gather | solution.py:427
  12.6 38.5 %all-gather.7.cloned.1.call-start = ((), (), s32[]{:S(2)}) async-start(), calls=%async_computation.9 | async-start | bytes 1310720 | tf_op jit(solution)/shard_map/all_gather | solution.py:428
  14.9 74.0 %all-gather.9.cloned.1.call-start = ((), (), s32[]{:S(2)}) async-start(), calls=%async_computation.10 | async-start | bytes 1310720 | tf_op jit(solution)/shard_map/all_gather | solution.py:429
  17.0 75.2 %all-gather.11.cloned.1.call-start = ((), (), s32[]{:S(2)}) async-start(), calls=%async_computation.11 | async-start | bytes 1310720 | tf_op jit(solution)/shard_map/all_gather | solution.py:430
  124.5 15.6 %all-to-all-start = ((bf16[2,4,96,512]{3,2,0,1:T(8,128)(2,1)}), bf16[2,4,96,512]{3,2,0,1:T(8,128)(2,1)S(1)}, u32[]{:S(2)}, u32[]{:S(2)}) async-start(bf16[2,4,96,512]{3,2,0,1:T(8,128)(2,1)} %copy.217), calls=%async_computation | async-start | bytes 1572864 | tf_op jit(solution)/shard_map/all_to_all | solution.py:457
  148.0 15.1 %all-to-all-start.1 = ((bf16[2,4,96,512]{3,2,0,1:T(8,128)(2,1)}), bf16[2,4,96,512]{3,2,0,1:T(8,128)(2,1)S(1)}, u32[]{:S(2)}, u32[]{:S(2)}) async-start(bf16[2,4,96,512]{3,2,0,1:T(8,128)(2,1)} %copy.219), calls=%async_computation.1 | async-start | bytes 1572864 | tf_op jit(solution)/shard_map/all_to_all | solution.py:466
  166.2 43.3 %collective-permute-start = (bf16[2,256,512]{2,1,0:T(8,128)(2,1)}, bf16[2,256,512]{2,1,0:T(8,128)(2,1)}, u32[]{:S(2)}, u32[]{:S(2)}) collective-permute-start(bf16[2,256,512]{2,1,0:T(8,128)(2,1)} %multiply_convert_fusion.6), channel_id=1, source_target_pairs={{0,1},{1,0},{2,3},{3,2},{4,5},{5,4},{6,7},{7,6},{8,9},{9,8},{10,11... | collective-permute-start | bytes 1572872 | tf_op jit(solution)/shard_map/ppermute | solution.py:27
  166.8 43.9 %collective-permute-start.1 = (bf16[2,256,512]{2,1,0:T(8,128)(2,1)}, bf16[2,256,512]{2,1,0:T(8,128)(2,1)}, u32[]{:S(2)}, u32[]{:S(2)}) collective-permute-start(bf16[2,256,512]{2,1,0:T(8,128)(2,1)} %multiply_convert_fusion.6), channel_id=1, source_target_pairs={{0,2},{1,3},{2,0},{3,1},{4,6},{5,7},{6,4},{7,5},{8,10},{9,11},{10,... | collective-permute-start | bytes 1572872 | tf_op jit(solution)/shard_map/ppermute | solution.py:27
  210.7 20.1 %collective-permute-start.2 = (bf16[2,256,512]{2,1,0:T(8,128)(2,1)}, bf16[2,256,512]{2,1,0:T(8,128)(2,1)}, u32[]{:S(2)}, u32[]{:S(2)}) collective-permute-start(bf16[2,256,512]{2,1,0:T(8,128)(2,1)} %collective-permute-done.1), channel_id=1, source_target_pairs={{0,1},{1,0},{2,3},{3,2},{4,5},{5,4},{6,7},{7,6},{8,9},{9,8},{10,11... | collective-permute-start | bytes 1572872 | tf_op jit(solution)/shard_map/ppermute | solution.py:27
  252.0 9.7 %collective-permute-start.3 = (f32[3,4,2,256]{3,2,1,0:T(2,128)S(1)}, f32[3,4,2,256]{3,2,1,0:T(2,128)S(1)}, u32[]{:S(2)}, u32[]{:S(2)}) collective-permute-start(f32[3,4,2,256]{3,2,1,0:T(2,128)S(1)} %bitcast.928), channel_id=1, source_target_pairs={{0,1},{1,0},{2,3},{3,2},{4,5},{5,4},{6,7},{7,6},{8,9},{9,8},{10,11... | collective-permute-start | bytes 73736 | tf_op jit(solution)/shard_map/ppermute | solution.py:27
  321.3 58.6 %collective-permute-start.34 = (bf16[2,64,2048]{2,1,0:T(8,128)(2,1)}, bf16[2,64,2048]{2,1,0:T(8,128)(2,1)}, u32[]{:S(2)}, u32[]{:S(2)}) collective-permute-start(bf16[2,64,2048]{2,1,0:T(8,128)(2,1)} %slice_bitcast_fusion.3), channel_id=1, source_target_pairs={{0,8},{4,12},{8,24},{12,28},{24,16},{28,20},{16,0},{20,4},{1,9},{5... | collective-permute-start | bytes 1572872 | tf_op jit(solution)/shard_map/ppermute | solution.py:87
  339.8 58.3 %collective-permute-start.38 = (bf16[4,64,2048]{2,1,0:T(8,128)(2,1)}, bf16[4,64,2048]{2,1,0:T(8,128)(2,1)S(1)}, u32[]{:S(2)}, u32[]{:S(2)}) collective-permute-start(bf16[4,64,2048]{2,1,0:T(8,128)(2,1)} %bitcast.238), channel_id=1, source_target_pairs={{0,4},{4,0},{8,12},{12,8},{16,20},{20,16},{24,28},{28,24},{1,5},{5... | collective-permute-start | bytes 3145736 | tf_op jit(solution)/shard_map/ppermute | solution.py:27
  358.2 44.0 %collective-permute-start.42 = (bf16[4,64,2048]{2,1,0:T(8,128)(2,1)}, bf16[4,64,2048]{2,1,0:T(8,128)(2,1)}, u32[]{:S(2)}, u32[]{:S(2)}) collective-permute-start(bf16[4,64,2048]{2,1,0:T(8,128)(2,1)} %bitcast.244), channel_id=1, source_target_pairs={{0,4},{4,0},{8,12},{12,8},{16,20},{20,16},{24,28},{28,24},{1,5},{5... | collective-permute-start | bytes 3145736 | tf_op jit(solution)/shard_map/ppermute | solution.py:27
  376.0 33.3 %collective-permute-start.46 = (bf16[4,64,2048]{2,1,0:T(8,128)(2,1)}, bf16[4,64,2048]{2,1,0:T(8,128)(2,1)}, u32[]{:S(2)}, u32[]{:S(2)}) collective-permute-start(bf16[4,64,2048]{2,1,0:T(8,128)(2,1)} %bitcast.250), channel_id=1, source_target_pairs={{0,4},{4,0},{8,12},{12,8},{16,20},{20,16},{24,28},{28,24},{1,5},{5... | collective-permute-start | bytes 3145736 | tf_op jit(solution)/shard_map/ppermute | solution.py:27
  381.1 15.1 %collective-permute-start.35 = (bf16[2,64,2048]{2,1,0:T(8,128)(2,1)S(1)}, bf16[2,64,2048]{2,1,0:T(8,128)(2,1)S(1)}, u32[]{:S(2)}, u32[]{:S(2)}) collective-permute-start(bf16[2,64,2048]{2,1,0:T(8,128)(2,1)S(1)} %fusion.136), channel_id=1, source_target_pairs={{0,8},{4,12},{8,24},{12,28},{24,16},{28,20},{16,0},{20,4},{1,9},{5... | collective-permute-start | bytes 1572872 | tf_op jit(solution)/shard_map/ppermute | solution.py:87
  387.2 26.2 %collective-permute-start.7 = (bf16[2,2,256,512]{3,2,1,0:T(8,128)(2,1)S(1)}, bf16[2,2,256,512]{3,2,1,0:T(8,128)(2,1)S(1)}, u32[]{:S(2)}, u32[]{:S(2)}) collective-permute-start(bf16[2,2,256,512]{3,2,1,0:T(8,128)(2,1)S(1)} %pad_maximum_fusion.4), channel_id=1, source_target_pairs={{0,1},{1,0},{2,3},{3,2},{4,5},{5,4},{6,7},{7,6},{8,9},{9,8},{10,11... | collective-permute-start | bytes 3145736 | tf_op jit(solution)/shard_map/ppermute | solution.py:27
  396.4 34.1 %collective-permute-start.36 = (bf16[2,64,2048]{2,1,0:T(8,128)(2,1)S(1)}, bf16[2,64,2048]{2,1,0:T(8,128)(2,1)S(1)}, u32[]{:S(2)}, u32[]{:S(2)}) collective-permute-start(bf16[2,64,2048]{2,1,0:T(8,128)(2,1)S(1)} %fusion.135), channel_id=1, source_target_pairs={{0,8},{4,12},{8,24},{12,28},{24,16},{28,20},{16,0},{20,4},{1,9},{5... | collective-permute-start | bytes 1572872 | tf_op jit(solution)/shard_map/ppermute | solution.py:87
  400.7 17.1 %collective-permute-start.39 = (bf16[64,2048]{1,0:T(8,128)(2,1)S(1)}, bf16[64,2048]{1,0:T(8,128)(2,1)S(1)}, u32[]{:S(2)}, u32[]{:S(2)}) collective-permute-start(bf16[64,2048]{1,0:T(8,128)(2,1)S(1)} %slice_bitcast_fusion.24), channel_id=1, source_target_pairs={{0,8},{4,12},{8,24},{12,28},{24,16},{28,20},{16,0},{20,4},{1,9},{5... | collective-permute-start | bytes 786440 | tf_op jit(solution)/shard_map/ppermute | solution.py:87
  403.9 19.6 %collective-permute-start.43 = (bf16[64,2048]{1,0:T(8,128)(2,1)S(1)}, bf16[64,2048]{1,0:T(8,128)(2,1)S(1)}, u32[]{:S(2)}, u32[]{:S(2)}) collective-permute-start(bf16[64,2048]{1,0:T(8,128)(2,1)S(1)} %slice_bitcast_fusion.20), channel_id=1, source_target_pairs={{0,8},{4,12},{8,24},{12,28},{24,16},{28,20},{16,0},{20,4},{1,9},{5... | collective-permute-start | bytes 786440 | tf_op jit(solution)/shard_map/ppermute | solution.py:87
  410.9 18.2 %collective-permute-start.47 = (bf16[64,2048]{1,0:T(8,128)(2,1)S(1)}, bf16[64,2048]{1,0:T(8,128)(2,1)S(1)}, u32[]{:S(2)}, u32[]{:S(2)}) collective-permute-start(bf16[64,2048]{1,0:T(8,128)(2,1)S(1)} %slice_bitcast_fusion.16), channel_id=1, source_target_pairs={{0,8},{4,12},{8,24},{12,28},{24,16},{28,20},{16,0},{20,4},{1,9},{5... | collective-permute-start | bytes 786440 | tf_op jit(solution)/shard_map/ppermute | solution.py:87
  413.6 18.4 %collective-permute-start.8 = (bf16[1,2,256,512]{3,2,1,0:T(8,128)(2,1)S(1)}, bf16[1,2,256,512]{3,2,1,0:T(8,128)(2,1)S(1)}, u32[]{:S(2)}, u32[]{:S(2)}) collective-permute-start(bf16[1,2,256,512]{3,2,1,0:T(8,128)(2,1)S(1)} %fusion.144), channel_id=1, source_target_pairs={{0,2},{1,3},{2,0},{3,1},{4,6},{5,7},{6,4},{7,5},{8,10},{9,11},{10,... | collective-permute-start | bytes 1572872 | tf_op jit(solution)/shard_map/ppermute | solution.py:27
  417.9 22.3 %collective-permute-start.40 = (bf16[64,2048]{1,0:T(8,128)(2,1)S(1)}, bf16[64,2048]{1,0:T(8,128)(2,1)}, u32[]{:S(2)}, u32[]{:S(2)}) collective-permute-start(bf16[64,2048]{1,0:T(8,128)(2,1)S(1)} %fusion.172), channel_id=1, source_target_pairs={{0,8},{4,12},{8,24},{12,28},{24,16},{28,20},{16,0},{20,4},{1,9},{5... | collective-permute-start | bytes 786440 | tf_op jit(solution)/shard_map/ppermute | solution.py:87
  424.2 19.5 %collective-permute-start.44 = (bf16[64,2048]{1,0:T(8,128)(2,1)}, bf16[64,2048]{1,0:T(8,128)(2,1)}, u32[]{:S(2)}, u32[]{:S(2)}) collective-permute-start(bf16[64,2048]{1,0:T(8,128)(2,1)} %fusion.169), channel_id=1, source_target_pairs={{0,8},{4,12},{8,24},{12,28},{24,16},{28,20},{16,0},{20,4},{1,9},{5... | collective-permute-start | bytes 786440 | tf_op jit(solution)/shard_map/ppermute | solution.py:87
  429.8 15.1 %collective-permute-start.48 = (bf16[64,2048]{1,0:T(8,128)(2,1)}, bf16[64,2048]{1,0:T(8,128)(2,1)}, u32[]{:S(2)}, u32[]{:S(2)}) collective-permute-start(bf16[64,2048]{1,0:T(8,128)(2,1)} %fusion.166), channel_id=1, source_target_pairs={{0,8},{4,12},{8,24},{12,28},{24,16},{28,20},{16,0},{20,4},{1,9},{5... | collective-permute-start | bytes 786440 | tf_op jit(solution)/shard_map/ppermute | solution.py:87
  431.4 16.6 %collective-permute-start.37 = (bf16[64,2048]{1,0:T(8,128)(2,1)}, bf16[64,2048]{1,0:T(8,128)(2,1)}, u32[]{:S(2)}, u32[]{:S(2)}) collective-permute-start(bf16[64,2048]{1,0:T(8,128)(2,1)} %slice_bitcast_fusion.25), channel_id=1, source_target_pairs={{0,4},{4,0},{8,12},{12,8},{16,20},{20,16},{24,28},{28,24},{1,5},{5... | collective-permute-start | bytes 786440 | tf_op jit(solution)/shard_map/ppermute | solution.py:27
  436.0 28.6 %all-to-all-start.2 = ((bf16[2,4,96,512]{3,2,0,1:T(8,128)(2,1)}), bf16[2,4,96,512]{3,2,0,1:T(8,128)(2,1)}, u32[]{:S(2)}, u32[]{:S(2)}) async-start(bf16[2,4,96,512]{3,2,0,1:T(8,128)(2,1)} %copy.248), calls=%async_computation.2 | async-start | bytes 1572864 | tf_op jit(solution)/shard_map/all_to_all | solution.py:570
  441.3 10.1 %collective-permute-start.41 = (bf16[64,2048]{1,0:T(8,128)(2,1)S(1)}, bf16[64,2048]{1,0:T(8,128)(2,1)S(1)}, u32[]{:S(2)}, u32[]{:S(2)}) collective-permute-start(bf16[64,2048]{1,0:T(8,128)(2,1)S(1)} %fusion.171), channel_id=1, source_target_pairs={{0,8},{4,12},{8,24},{12,28},{24,16},{28,20},{16,0},{20,4},{1,9},{5... | collective-permute-start | bytes 786440 | tf_op jit(solution)/shard_map/ppermute | solution.py:87
  444.8 12.2 %collective-permute-start.45 = (bf16[64,2048]{1,0:T(8,128)(2,1)S(1)}, bf16[64,2048]{1,0:T(8,128)(2,1)S(1)}, u32[]{:S(2)}, u32[]{:S(2)}) collective-permute-start(bf16[64,2048]{1,0:T(8,128)(2,1)S(1)} %fusion.168), channel_id=1, source_target_pairs={{0,8},{4,12},{8,24},{12,28},{24,16},{28,20},{16,0},{20,4},{1,9},{5... | collective-permute-start | bytes 786440 | tf_op jit(solution)/shard_map/ppermute | solution.py:87
  446.0 16.2 %collective-permute-start.49 = (bf16[64,2048]{1,0:T(8,128)(2,1)S(1)}, bf16[64,2048]{1,0:T(8,128)(2,1)S(1)}, u32[]{:S(2)}, u32[]{:S(2)}) collective-permute-start(bf16[64,2048]{1,0:T(8,128)(2,1)S(1)} %fusion.165), channel_id=1, source_target_pairs={{0,8},{4,12},{8,24},{12,28},{24,16},{28,20},{16,0},{20,4},{1,9},{5... | collective-permute-start | bytes 786440 | tf_op jit(solution)/shard_map/ppermute | solution.py:87
  476.7 15.1 %all-to-all-start.3 = ((bf16[2,4,96,512]{3,2,0,1:T(8,128)(2,1)}), bf16[2,4,96,512]{3,2,0,1:T(8,128)(2,1)S(1)}, u32[]{:S(2)}, u32[]{:S(2)}) async-start(bf16[2,4,96,512]{3,2,0,1:T(8,128)(2,1)} %copy.250), calls=%async_computation.3 | async-start | bytes 1572864 | tf_op jit(solution)/shard_map/all_to_all | solution.py:586
  480.2 202.8 %reduce-scatter.9.cloned.1.call-start = ((), (), s32[]{:S(2)}) async-start(), calls=%async_computation.14 | async-start | bytes 1310720 | tf_op jit(solution)/shard_map/reduce_scatter | solution.py:627
  486.3 156.5 %collective-permute-start.30 = (bf16[4,256,512]{2,1,0:T(8,128)(2,1)}, bf16[4,256,512]{2,1,0:T(8,128)(2,1)}, u32[]{:S(2)}, u32[]{:S(2)}) collective-permute-start(bf16[4,256,512]{2,1,0:T(8,128)(2,1)} %pad_maximum_fusion.8), channel_id=1, source_target_pairs={{0,4},{4,0},{8,12},{12,8},{16,20},{20,16},{24,28},{28,24},{1,5},{5... | collective-permute-start | bytes 3145736 | tf_op jit(solution)/shard_map/ppermute | solution.py:27
  558.5 126.5 %reduce-scatter.11.cloned.1.call-start = ((), (), s32[]{:S(2)}) async-start(), calls=%async_computation.15 | async-start | bytes 1310720 | tf_op jit(solution)/shard_map/reduce_scatter | solution.py:630
  564.8 81.3 %collective-permute-start.26 = (bf16[4,64,2048]{2,1,0:T(8,128)(2,1)}, bf16[4,64,2048]{2,1,0:T(8,128)(2,1)}, u32[]{:S(2)}, u32[]{:S(2)}) collective-permute-start(bf16[4,64,2048]{2,1,0:T(8,128)(2,1)} %pad_maximum_fusion.7), channel_id=1, source_target_pairs={{0,4},{4,0},{8,12},{12,8},{16,20},{20,16},{24,28},{28,24},{1,5},{5... | collective-permute-start | bytes 3145736 | tf_op jit(solution)/shard_map/ppermute | solution.py:27
  568.5 121.1 %reduce-scatter.5.cloned.1.call-start = ((), (), s32[]{:S(2)}) async-start(), calls=%async_computation.12 | async-start | bytes 1310720 | tf_op jit(solution)/shard_map/reduce_scatter | solution.py:621
  638.1 53.7 %reduce-scatter.7.cloned.1.call-start = ((), (), s32[]{:S(2)}) async-start(), calls=%async_computation.13 | async-start | bytes 1310720 | tf_op jit(solution)/shard_map/reduce_scatter | solution.py:624
  644.6 10.2 %collective-permute-start.31 = (bf16[256,512]{1,0:T(8,128)(2,1)S(1)}, bf16[256,512]{1,0:T(8,128)(2,1)S(1)}, u32[]{:S(2)}, u32[]{:S(2)}) collective-permute-start(bf16[256,512]{1,0:T(8,128)(2,1)S(1)} %slice_bitcast_fusion.30), channel_id=1, source_target_pairs={{0,8},{4,12},{8,24},{12,28},{24,16},{28,20},{16,0},{20,4},{1,9},{5... | collective-permute-start | bytes 786440 | tf_op jit(solution)/shard_map/ppermute | solution.py:87
  647.8 12.6 %collective-permute-start.27 = (bf16[64,2048]{1,0:T(8,128)(2,1)S(1)}, bf16[64,2048]{1,0:T(8,128)(2,1)S(1)}, u32[]{:S(2)}, u32[]{:S(2)}) collective-permute-start(bf16[64,2048]{1,0:T(8,128)(2,1)S(1)} %slice_bitcast_fusion.34), channel_id=1, source_target_pairs={{0,8},{4,12},{8,24},{12,28},{24,16},{28,20},{16,0},{20,4},{1,9},{5... | collective-permute-start | bytes 786440 | tf_op jit(solution)/shard_map/ppermute | solution.py:87
  655.6 10.6 %collective-permute-start.32 = (bf16[256,512]{1,0:T(8,128)(2,1)}, bf16[256,512]{1,0:T(8,128)(2,1)}, u32[]{:S(2)}, u32[]{:S(2)}) collective-permute-start(bf16[256,512]{1,0:T(8,128)(2,1)} %fusion.176), channel_id=1, source_target_pairs={{0,8},{4,12},{8,24},{12,28},{24,16},{28,20},{16,0},{20,4},{1,9},{5... | collective-permute-start | bytes 786440 | tf_op jit(solution)/shard_map/ppermute | solution.py:87
  661.2 10.6 %collective-permute-start.28 = (bf16[64,2048]{1,0:T(8,128)(2,1)}, bf16[64,2048]{1,0:T(8,128)(2,1)}, u32[]{:S(2)}, u32[]{:S(2)}) collective-permute-start(bf16[64,2048]{1,0:T(8,128)(2,1)} %fusion.179), channel_id=1, source_target_pairs={{0,8},{4,12},{8,24},{12,28},{24,16},{28,20},{16,0},{20,4},{1,9},{5... | collective-permute-start | bytes 786440 | tf_op jit(solution)/shard_map/ppermute | solution.py:87
  667.3 10.2 %collective-permute-start.33 = (bf16[256,512]{1,0:T(8,128)(2,1)S(1)}, bf16[256,512]{1,0:T(8,128)(2,1)S(1)}, u32[]{:S(2)}, u32[]{:S(2)}) collective-permute-start(bf16[256,512]{1,0:T(8,128)(2,1)S(1)} %fusion.175), channel_id=1, source_target_pairs={{0,8},{4,12},{8,24},{12,28},{24,16},{28,20},{16,0},{20,4},{1,9},{5... | collective-permute-start | bytes 786440 | tf_op jit(solution)/shard_map/ppermute | solution.py:87
  672.9 8.3 %collective-permute-start.29 = (bf16[64,2048]{1,0:T(8,128)(2,1)S(1)}, bf16[64,2048]{1,0:T(8,128)(2,1)S(1)}, u32[]{:S(2)}, u32[]{:S(2)}) collective-permute-start(bf16[64,2048]{1,0:T(8,128)(2,1)S(1)} %fusion.178), channel_id=1, source_target_pairs={{0,8},{4,12},{8,24},{12,28},{24,16},{28,20},{16,0},{20,4},{1,9},{5... | collective-permute-start | bytes 786440 | tf_op jit(solution)/shard_map/ppermute | solution.py:87
  689.7 21.0 %collective-permute-start.20 = (bf16[2,4,512,128]{3,2,1,0:T(8,128)(2,1)}, bf16[2,4,512,128]{3,2,1,0:T(8,128)(2,1)}, u32[]{:S(2)}, u32[]{:S(2)}) collective-permute-start(bf16[2,4,512,128]{3,2,1,0:T(8,128)(2,1)} %pad_maximum_fusion.6), channel_id=1, source_target_pairs={{0,1},{1,0},{2,3},{3,2},{4,5},{5,4},{6,7},{7,6},{8,9},{9,8},{10,11... | collective-permute-start | bytes 3145736 | tf_op jit(solution)/shard_map/ppermute | solution.py:27
  698.0 16.4 %collective-permute-start.14 = (bf16[2,4,512,128]{3,2,1,0:T(8,128)(2,1)S(1)}, bf16[2,4,512,128]{3,2,1,0:T(8,128)(2,1)S(1)}, u32[]{:S(2)}, u32[]{:S(2)}) collective-permute-start(bf16[2,4,512,128]{3,2,1,0:T(8,128)(2,1)S(1)} %pad_maximum_fusion.5), channel_id=1, source_target_pairs={{0,1},{1,0},{2,3},{3,2},{4,5},{5,4},{6,7},{7,6},{8,9},{9,8},{10,11... | collective-permute-start | bytes 3145736 | tf_op jit(solution)/shard_map/ppermute | solution.py:27
  711.9 14.9 %collective-permute-start.21 = (bf16[1,4,512,128]{3,2,1,0:T(8,128)(2,1)S(1)}, bf16[1,4,512,128]{3,2,1,0:T(8,128)(2,1)S(1)}, u32[]{:S(2)}, u32[]{:S(2)}) collective-permute-start(bf16[1,4,512,128]{3,2,1,0:T(8,128)(2,1)S(1)} %fusion.161), channel_id=1, source_target_pairs={{0,2},{1,3},{2,0},{3,1},{4,6},{5,7},{6,4},{7,5},{8,10},{9,11},{10,... | collective-permute-start | bytes 1572872 | tf_op jit(solution)/shard_map/ppermute | solution.py:27
  714.6 19.3 %collective-permute-start.15 = (bf16[1,4,512,128]{3,2,1,0:T(8,128)(2,1)S(1)}, bf16[1,4,512,128]{3,2,1,0:T(8,128)(2,1)S(1)}, u32[]{:S(2)}, u32[]{:S(2)}) collective-permute-start(bf16[1,4,512,128]{3,2,1,0:T(8,128)(2,1)S(1)} %fusion.160), channel_id=1, source_target_pairs={{0,2},{1,3},{2,0},{3,1},{4,6},{5,7},{6,4},{7,5},{8,10},{9,11},{10,... | collective-permute-start | bytes 1572872 | tf_op jit(solution)/shard_map/ppermute | solution.py:27
  728.2 8.2 %collective-permute-start.22 = (bf16[4,4,64,128]{3,2,1,0:T(8,128)(2,1)S(1)}, bf16[4,4,64,128]{3,2,1,0:T(8,128)(2,1)S(1)}, u32[]{:S(2)}, u32[]{:S(2)}) collective-permute-start(bf16[4,4,64,128]{3,2,1,0:T(8,128)(2,1)S(1)} %pad_maximum_fusion.13), channel_id=1, source_target_pairs={{0,4},{4,0},{8,12},{12,8},{16,20},{20,16},{24,28},{28,24},{1,5},{5... | collective-permute-start | bytes 786440 | tf_op jit(solution)/shard_map/ppermute | solution.py:27
  734.2 6.4 collective-permute-start.16
  (118 other events, 857.3 us)
Sparse Core Ops, SparseCore 0:
  12.7 19.4 all-gather.4
  34.3 16.7 all-gather.6
  53.2 16.7 all-gather.8
  71.9 16.8 all-gather.10
  558.7 23.6 reduce-scatter.8
  584.9 24.8 reduce-scatter.10
  638.3 22.7 reduce-scatter.4
  663.7 24.8 reduce-scatter.6
